TPU v7x, 32 devices: a whole 2x2x4 slice. The times are simulated.
32 devices in a mesh: rows: 8 (over z, x), grp: 4 (over y, core).
Axes of the slice: x: 2, y: 2, z: 4, core: 2. Of those that a mesh axis runs over, the one named last changes fastest.
Arguments:
- a_blocks: float32 [256, 7, 128, 128], P(('rows', 'grp')), may hold values from -0.5 to 0.5
- neighbours: int32 [256, 7], P(('rows', 'grp')), may hold values from 0 to 255, as said below
- neighbour_count: int32 [256], P(('rows', 'grp')), may hold values from 1 to 7
- p_blocks: float32 [256, 2, 128, 128], P(('rows', 'grp')), may hold values from -1 to 1
- p_columns: int32 [256, 2], P(('rows', 'grp')), may hold values from 0 to 31, as said below
- p_count: int32 [256], P(('rows', 'grp')), may hold values from 1 to 2
- coarse_slot: int32 [32], replicated, may hold values from 0 to 3, as said below
- coarse_pattern: int32 [32, 4], replicated, may hold values from 0 to 31, as said below
Outputs:
- coarse_op: float32 [32, 4, 128, 128], P(('rows', 'grp'))
Inputs may be any that keep to these rules, and one draw needn't show every extreme that they name: neighbours[e,0] = e; every neighbour of an element of the slab of 32 elements that holds it lies in that slab or within 8 elements before or after it. The elements of slab q form aggregates q * 4 to (q + 1) * 4 - 1, eight elements each; p_columns[e,0] is the aggregate of e, and every slot names an aggregate of the element's slab or of a slab beside it. `coarse_slot`: within each slab the aggregates take each position 0 to 3 once. coarse_pattern[c,0] = c; every column is an aggregate of c's slab or of a slab beside it; columns may repeat.
All inputs are finite; a program needn't handle non-finite values.
Results may differ from a plain program's by a relative error of at most 0.0003.
Values sent between devices are 32-bit elements; how exact they have to be, the bound alone decides.
No kernel may reach another device: no remote copies, remote signals or barrier semaphores. Data moves between devices by JAX's collectives and lax.ppermute only.
A program may use at most 64 MiB of HBM per device.

v0:
```python
import jax
import jax.numpy as jnp
from jax import lax
from jax.sharding import PartitionSpec as P

HIGH = lax.Precision.HIGHEST


def shifted(value, axis, steps):
    count = lax.axis_size(axis)
    initial, last = (max(0, -steps), min(count, count - steps))
    return lax.ppermute(value, axis, [(source, source + steps) for source in range(initial, last)])


def per_device(
    a_blocks, neighbours, neighbour_count, p_blocks, p_columns, p_count, coarse_slot, coarse_pattern
):
    groups = lax.axis_size("grp")
    e_local = a_blocks.shape[0]
    slab_len = groups * e_local
    agg_slab = slab_len // 8
    n_slot = a_blocks.shape[1]
    p_slot = p_blocks.shape[1]
    row_index = lax.axis_index("rows")
    slab_p, slab_cols, slab_count = (
        lax.all_gather(p_blocks, "grp", axis=0, tiled=True),
        lax.all_gather(p_columns, "grp", axis=0, tiled=True),
        lax.all_gather(p_count, "grp", axis=0, tiled=True),
    )
    prev_p, prev_cols, prev_count = shifted(
        (
            slab_p[slab_len - e_local :],
            slab_cols[slab_len - e_local :],
            slab_count[slab_len - e_local :],
        ),
        "rows",
        1,
    )
    next_p, next_cols, next_count = shifted(
        (slab_p[:e_local], slab_cols[:e_local], slab_count[:e_local]), "rows", -1
    )
    wide_p = jnp.concatenate([prev_p, slab_p, next_p], axis=0)
    wide_cols = jnp.concatenate([prev_cols, slab_cols, next_cols], axis=0)
    wide_count = jnp.concatenate([prev_count, slab_count, next_count], axis=0)
    base_row = row_index * slab_len - e_local
    local_near = neighbours - base_row
    near_p = jnp.take(wide_p, local_near, axis=0)
    near_cols = jnp.take(wide_cols, local_near, axis=0)
    near_live = (
        jnp.arange(p_slot, dtype=jnp.int32)[None, None, :]
        < jnp.take(wide_count, local_near, axis=0)[:, :, None]
    )
    slot_live = jnp.arange(n_slot, dtype=jnp.int32)[None, :] < neighbour_count[:, None]
    own_live = jnp.arange(p_slot, dtype=jnp.int32)[None, :] < p_count[:, None]
    products = jnp.einsum("ekab,ekjbc->ekjac", a_blocks, near_p, precision=HIGH)
    targets = jnp.take(coarse_pattern, p_columns, axis=0)
    select = (
        slot_live[:, None, None, :, None]
        & own_live[:, :, None, None, None]
        & near_live[:, None, None, :, :]
        & (near_cols[:, None, None, :, :] == targets[:, :, :, None, None])
    ).astype(jnp.float32)
    summed = jnp.einsum("ejskl,eklac->ejsac", select, products, precision=HIGH)
    terms = jnp.einsum("ejba,ejsbc->ejsac", p_blocks, summed, precision=HIGH)
    slab_offset = p_columns // agg_slab - row_index + 1
    position = slab_offset * agg_slab + jnp.take(coarse_slot, p_columns, axis=0)
    onehot = (
        position[:, :, None] == jnp.arange(3 * agg_slab, dtype=jnp.int32)[None, None, :]
    ).astype(jnp.float32)
    partial_value = jnp.einsum("ejt,ejsac->tsac", onehot, terms, precision=HIGH)
    from_next = shifted(partial_value[:agg_slab], "rows", -1)
    from_prev = shifted(partial_value[2 * agg_slab :], "rows", 1)
    mine = partial_value[agg_slab : 2 * agg_slab] + from_next + from_prev
    result = lax.psum_scatter(mine, "grp", scatter_dimension=0, tiled=True)
    return result


def solution(mesh):
    return jax.shard_map(
        per_device,
        mesh=mesh,
        in_specs=(
            P(("rows", "grp"), None, None, None),
            P(("rows", "grp"), None),
            P(("rows", "grp")),
            P(("rows", "grp"), None, None, None),
            P(("rows", "grp"), None),
            P(("rows", "grp")),
            P(),
            P(),
        ),
        out_specs=P(("rows", "grp"), None, None, None),
        check_vma=False,
    )
```

profile of v0, /device:TPU:0, one launch (start us, length us, event | category | flops | bytes accessed | tf_op | source)
XLA Modules:
  0.0 251.3 jit_solution(6312327893982298415)
XLA Ops:
  10.1 6.4 %all-reduce = s32[32]{0:T(128)S(1)} all-reduce(s32[32]{0:T(128)S(1)} %dynamic-update-slice), channel_id=1, replica_groups=mesh['rows'=8,'grp'=4] {'grp'}, use_global_device_ids=true, to_apply=%add | all-reduce | flops 32 | bytes 256
  16.5 3.4 %collective-permute-start = (s32[8]{0:T(128)S(1)}, s32[8]{0:T(128)S(1)}, u32[]{:S(2)}, u32[]{:S(2)}) collective-permute-start(s32[8]{0:T(128)S(1)} %get-tuple-element.13), channel_id=1, source_target_pairs={{0,4},{4,8},{8,12},{12,16},{16,20},{20,24},{24,28},{1,5},{5,9},{9,... | collective-permute-start | bytes 104 | tf_op jit(solution)/shard_map/ppermute | solution.py:12
  19.9 1.3 collective-permute-start.1
  21.2 5.3 %all-gather = s32[4,8,2]{1,2,0:T(2,128)S(1)} all-gather(s32[1,8,2]{1,2,0:T(2,128)} %bitcast.50), channel_id=1, replica_groups=mesh['rows'=8,'grp'=4] {'grp'}, dimensions={0}, use_global_device_ids=true | all-gather | bytes 320 | tf_op jit(solution)/shard_map/all_gather | solution.py:27
  26.5 4.5 %collective-permute-start.2 = (s32[8,2]{0,1:T(2,128)S(1)}, s32[8,2]{0,1:T(2,128)S(1)}, u32[]{:S(2)}, u32[]{:S(2)}) collective-permute-start(s32[8,2]{0,1:T(2,128)S(1)} %get-tuple-element.11), channel_id=1, source_target_pairs={{0,4},{4,8},{8,12},{12,16},{16,20},{20,24},{24,28},{1,5},{5,9},{9,... | collective-permute-start | bytes 200 | tf_op jit(solution)/shard_map/ppermute | solution.py:12
  31.1 1.3 collective-permute-start.3
  36.6 9.6 %all-gather.3.cloned.1.call-done = f32[32,2,128,128]{3,2,1,0:T(8,128)} async-done(((f32[8,2,128,128]{3,2,1,0:T(8,128)}), f32[32,2,128,128]{3,2,1,0:T(8,128)}) %all-gather.3.cloned.1.call-update) | async-done | bytes 4194320 | tf_op jit(solution)/shard_map/all_gather | solution.py:26
  46.2 2.7 %fusion.34 = (f32[8,2,128,128]{3,2,1,0:T(8,128)}, f32[8,2,128,128]{3,2,1,0:T(8,128)S(1)}) fusion(f32[32,2,128,128]{3,2,1,0:T(8,128)} %all-gather.3.cloned.1.call-done), kind=kLoop, calls=%fused_computation.60 | loop fusion | bytes 4194304 | tf_op jit(solution)/shard_map/slice | solution.py:32
  48.9 3.4 %collective-permute-start.4 = (f32[8,2,128,128]{3,2,1,0:T(8,128)}, f32[8,2,128,128]{3,2,1,0:T(8,128)S(1)}, u32[]{:S(2)}, u32[]{:S(2)}) collective-permute-start(f32[8,2,128,128]{3,2,1,0:T(8,128)} %get-tuple-element.9), channel_id=1, source_target_pairs={{0,4},{4,8},{8,12},{12,16},{16,20},{20,24},{24,28},{1,5},{5,9},{9,... | collective-permute-start | bytes 3145736 | tf_op jit(solution)/shard_map/ppermute | solution.py:12
  52.3 1.3 collective-permute-start.5
  55.6 42.3 %collective-permute-done.4 = f32[8,2,128,128]{3,2,1,0:T(8,128)S(1)} collective-permute-done((f32[8,2,128,128]{3,2,1,0:T(8,128)}, f32[8,2,128,128]{3,2,1,0:T(8,128)S(1)}, u32[]{:S(2)}, u32[]{:S(2)}) %collective-permute-start.4) | collective-permute-done | bytes 1048608 | tf_op jit(solution)/shard_map/ppermute | solution.py:12
  97.9 5.9 %pad_maximum_fusion = f32[48,2,128,128]{3,2,1,0:T(8,128)} fusion(f32[8,2,128,128]{3,2,1,0:T(8,128)S(1)} %collective-permute-done.5, f32[32,2,128,128]{3,2,1,0:T(8,128)} %all-gather.3.cloned.1.call-done, f32[8,2,128,128]{3,2,1,0:T(8,128)S(1)} %collective-permute-done.4), kind=kLoop, calls=%fused_computation.7 | loop fusion | flops 3145728 | bytes 12582912 | tf_op jit(solution)/shard_map/concatenate | solution.py:42
  103.8 6.7 %gather_fusion.4 = f32[56,2,128,128]{3,2,1,0:T(8,128)} fusion(f32[48,2,128,128]{3,2,1,0:T(8,128)} %pad_maximum_fusion, s32[1024]{0:T(1024)S(1)} %pad_clamp_fusion), kind=kCustom, calls=%fused_computation.4 | custom fusion | bytes 14680288 | tf_op jit(solution)/shard_map/jit(_take)/gather | solution.py:47
  110.5 8.5 %copy.51 = f32[8,7,2,128,128]{3,4,2,1,0:T(8,128)} copy(f32[8,7,2,128,128]{4,3,2,1,0:T(8,128)} %bitcast.48) | data formatting | bytes 14680064 | tf_op jit(solution)/shard_map/jit(_take)/gather | solution.py:47
  119.0 11.4 %fusion.7 = f32[8,7,2,128,128,1]{3,4,2,1,0,5:T(8,128)} fusion(f32[8,7,128,128]{3,2,1,0:T(8,128)} %param.8, f32[8,7,2,128,128]{3,4,2,1,0:T(8,128)} %copy.51, pred[8,7]{1,0:T(8,128)(4,1)S(1)} %get-tuple-element.6), kind=kOutput, calls=%fused_computation.13 | convolution fusion | flops 2820407296 | bytes 18350136 | tf_op jit(solution)/shard_map/ekab,ekjbc->ekjac/dot_general | solution.py:55
  130.5 8.9 %copy.58 = f32[8,7,2,128,128,1]{4,1,2,3,5,0:T(8,128)} copy(f32[8,7,2,128,128,1]{3,4,2,1,0,5:T(8,128)} %fusion.7) | data formatting | bytes 14680064 | tf_op jit(solution)/shard_map/ekab,ekjbc->ekjac/transpose | solution.py:55
  139.3 9.9 %convolution_bitcast_fusion.1 = f32[8,2,4,128,128]{4,2,3,1,0:T(4,128)S(1)} fusion(f32[8,7,2,128,128,1]{4,1,2,3,5,0:T(8,128)} %copy.58, s32[8,2,4]{2,1,0:T(2,128)S(1)} %broadcast_select_fusion, s32[8,7,2]{1,2,0:T(2,128)S(1)} %copy.49, pred[8,2,7,2]{2,3,1,0:T(4,128)(4,1)S(1)} %broadcast_and_fusion), kind=kOutput, calls=%fused_computation.15 | convolution fusion | flops 176162560 | bytes 11535264 | tf_op jit(solution)/shard_map/ejskl,eklac->ejsac/dot_general | solution.py:63
  149.3 8.4 %fusion.12 = f32[8,2,4,128,128]{3,4,2,1,0:T(8,128)} fusion(f32[8,2,4,128,128]{4,2,3,1,0:T(4,128)S(1)} %convolution_bitcast_fusion.1, f32[8,2,128,128]{3,2,1,0:T(8,128)S(1)} %copy-done.2), kind=kOutput, calls=%fused_computation.16 | convolution fusion | flops 1610612736 | bytes 9437184 | tf_op jit(solution)/shard_map/ejba,ejsbc->ejsac/dot_general | solution.py:64
  157.7 5.5 %copy.54 = f32[8,2,4,128,128]{4,0,1,3,2:T(8,128)} copy(f32[8,2,4,128,128]{3,4,2,1,0:T(8,128)} %fusion.12) | data formatting | bytes 8388608 | tf_op jit(solution)/shard_map/ejba,ejsbc->ejsac/transpose | solution.py:64
  163.3 4.0 %convolution_bitcast_fusion = f32[12,4,128,128]{3,0,2,1:T(8,128)S(1)} fusion(f32[8,2,4,128,128]{4,0,1,3,2:T(8,128)} %copy.54, s32[8,2]{0,1:T(2,128)S(1)} %copy.45), kind=kOutput, calls=%fused_computation.14 | convolution fusion | flops 150995136 | bytes 7340096 | tf_op jit(solution)/shard_map/ejt,ejsac->tsac/dot_general | solution.py:70
  168.9 5.0 %collective-permute-start.7 = (f32[4,4,128,128]{3,0,2,1:T(4,128)S(1)}, f32[4,4,128,128]{3,0,2,1:T(4,128)S(1)}, u32[]{:S(2)}, u32[]{:S(2)}) collective-permute-start(f32[4,4,128,128]{3,0,2,1:T(4,128)S(1)} %get-tuple-element.8), channel_id=1, source_target_pairs={{0,4},{4,8},{8,12},{12,16},{16,20},{20,24},{24,28},{1,5},{5,9},{9,... | collective-permute-start | bytes 3145736 | tf_op jit(solution)/shard_map/ppermute | solution.py:12
  173.8 20.7 %collective-permute-done.6 = f32[4,4,128,128]{3,0,2,1:T(4,128)S(1)} collective-permute-done((f32[4,4,128,128]{3,0,2,1:T(4,128)S(1)}, f32[4,4,128,128]{3,0,2,1:T(4,128)S(1)}, u32[]{:S(2)}, u32[]{:S(2)}) %collective-permute-start.6) | collective-permute-done | bytes 1048608 | tf_op jit(solution)/shard_map/ppermute | solution.py:12
  194.6 22.9 %collective-permute-done.7 = f32[4,4,128,128]{3,0,2,1:T(4,128)S(1)} collective-permute-done((f32[4,4,128,128]{3,0,2,1:T(4,128)S(1)}, f32[4,4,128,128]{3,0,2,1:T(4,128)S(1)}, u32[]{:S(2)}, u32[]{:S(2)}) %collective-permute-start.7) | collective-permute-done | bytes 1048608 | tf_op jit(solution)/shard_map/ppermute | solution.py:12
  219.1 25.4 %reduce-scatter.2.cloned.1.call-done = f32[1,4,128,128]{3,2,1,0:T(8,128)} async-done(((f32[4,4,128,128]{3,2,1,0:T(8,128)}), f32[1,4,128,128]{3,2,1,0:T(8,128)}) %reduce-scatter.2.cloned.1.call-update) | async-done | bytes 262160 | tf_op jit(solution)/shard_map/reduce_scatter | solution.py:74
  (63 shorter events, 12.2 us)
Async XLA Ops:
  6.5 28.9 %copy-start = (s32[32]{0:T(128)S(1)}, s32[32]{0:T(128)}, u32[]{:S(2)}) copy-start(s32[32]{0:T(128)} %param.14) | copy-start | bytes 388
  6.5 29.7 %copy-start.4 = (s32[8]{0:T(128)S(1)}, s32[8]{0:T(128)}, u32[]{:S(2)}) copy-start(s32[8]{0:T(128)} %param.13) | copy-start | bytes 100
  6.5 29.8 %copy-start.5 = (s32[8]{0:T(128)S(1)}, s32[8]{0:T(128)}, u32[]{:S(2)}) copy-start(s32[8]{0:T(128)} %param.10) | copy-start | bytes 100
  6.5 39.7 %all-gather.3.cloned.1.call-start = ((), (), s32[]{:S(2)}) async-start(), calls=%async_computation.1 | async-start | bytes 5242880 | tf_op jit(solution)/shard_map/all_gather | solution.py:26
  7.3 237.2 %reduce-scatter.2.cloned.1.call-start = ((), (), s32[]{:S(2)}) async-start(), calls=%async_computation.2 | async-start | bytes 1310720 | tf_op jit(solution)/shard_map/reduce_scatter | solution.py:74
  16.5 35.8 %collective-permute-start = (s32[8]{0:T(128)S(1)}, s32[8]{0:T(128)S(1)}, u32[]{:S(2)}, u32[]{:S(2)}) collective-permute-start(s32[8]{0:T(128)S(1)} %get-tuple-element.13), channel_id=1, source_target_pairs={{0,4},{4,8},{8,12},{12,16},{16,20},{20,24},{24,28},{1,5},{5,9},{9,... | collective-permute-start | bytes 104 | tf_op jit(solution)/shard_map/ppermute | solution.py:12
  19.9 33.7 %collective-permute-start.1 = (s32[8]{0:T(128)S(1)}, s32[8]{0:T(128)S(1)}, u32[]{:S(2)}, u32[]{:S(2)}) collective-permute-start(s32[8]{0:T(128)S(1)} %get-tuple-element.14), channel_id=1, source_target_pairs={{4,0},{8,4},{12,8},{16,12},{20,16},{24,20},{28,24},{5,1},{9,5},{13... | collective-permute-start | bytes 104 | tf_op jit(solution)/shard_map/ppermute | solution.py:12
  26.5 28.1 %collective-permute-start.2 = (s32[8,2]{0,1:T(2,128)S(1)}, s32[8,2]{0,1:T(2,128)S(1)}, u32[]{:S(2)}, u32[]{:S(2)}) collective-permute-start(s32[8,2]{0,1:T(2,128)S(1)} %get-tuple-element.11), channel_id=1, source_target_pairs={{0,4},{4,8},{8,12},{12,16},{16,20},{20,24},{24,28},{1,5},{5,9},{9,... | collective-permute-start | bytes 200 | tf_op jit(solution)/shard_map/ppermute | solution.py:12
  31.1 23.6 %collective-permute-start.3 = (s32[8,2]{0,1:T(2,128)S(1)}, s32[8,2]{0,1:T(2,128)S(1)}, u32[]{:S(2)}, u32[]{:S(2)}) collective-permute-start(s32[8,2]{0,1:T(2,128)S(1)} %get-tuple-element.12), channel_id=1, source_target_pairs={{4,0},{8,4},{12,8},{16,12},{20,16},{24,20},{28,24},{5,1},{9,5},{13... | collective-permute-start | bytes 200 | tf_op jit(solution)/shard_map/ppermute | solution.py:12
  36.6 18.0 %copy-start.3 = (s32[8,7]{1,0:T(8,128)S(1)}, s32[8,7]{1,0:T(8,128)}, u32[]{:S(2)}) copy-start(s32[8,7]{1,0:T(8,128)} %param.9) | copy-start | bytes 676
  48.9 49.0 %collective-permute-start.4 = (f32[8,2,128,128]{3,2,1,0:T(8,128)}, f32[8,2,128,128]{3,2,1,0:T(8,128)S(1)}, u32[]{:S(2)}, u32[]{:S(2)}) collective-permute-start(f32[8,2,128,128]{3,2,1,0:T(8,128)} %get-tuple-element.9), channel_id=1, source_target_pairs={{0,4},{4,8},{8,12},{12,16},{16,20},{20,24},{24,28},{1,5},{5,9},{9,... | collective-permute-start | bytes 3145736 | tf_op jit(solution)/shard_map/ppermute | solution.py:12
  52.3 45.5 %collective-permute-start.5 = (f32[8,2,128,128]{3,2,1,0:T(8,128)S(1)}, f32[8,2,128,128]{3,2,1,0:T(8,128)S(1)}, u32[]{:S(2)}, u32[]{:S(2)}) collective-permute-start(f32[8,2,128,128]{3,2,1,0:T(8,128)S(1)} %get-tuple-element.10), channel_id=1, source_target_pairs={{4,0},{8,4},{12,8},{16,12},{20,16},{24,20},{28,24},{5,1},{9,5},{13... | collective-permute-start | bytes 3145736 | tf_op jit(solution)/shard_map/ppermute | solution.py:12
  139.3 10.0 %copy-start.2 = (f32[8,2,128,128]{3,2,1,0:T(8,128)S(1)}, f32[8,2,128,128]{3,2,1,0:T(8,128)}, u32[]{:S(2)}) copy-start(f32[8,2,128,128]{3,2,1,0:T(8,128)} %param.11) | copy-start | bytes 3145732
  167.3 77.2 %copy-start.1 = (s32[32]{0:T(128)S(1)}, s32[32]{0:T(128)}, u32[]{:S(2)}) copy-start(s32[32]{0:T(128)} %param.14) | copy-start | bytes 388
  167.6 27.0 %collective-permute-start.6 = (f32[4,4,128,128]{3,0,2,1:T(4,128)S(1)}, f32[4,4,128,128]{3,0,2,1:T(4,128)S(1)}, u32[]{:S(2)}, u32[]{:S(2)}) collective-permute-start(f32[4,4,128,128]{3,0,2,1:T(4,128)S(1)} %get-tuple-element.7), channel_id=1, source_target_pairs={{4,0},{8,4},{12,8},{16,12},{20,16},{24,20},{28,24},{5,1},{9,5},{13... | collective-permute-start | bytes 3145736 | tf_op jit(solution)/shard_map/ppermute | solution.py:12
  168.9 48.7 %collective-permute-start.7 = (f32[4,4,128,128]{3,0,2,1:T(4,128)S(1)}, f32[4,4,128,128]{3,0,2,1:T(4,128)S(1)}, u32[]{:S(2)}, u32[]{:S(2)}) collective-permute-start(f32[4,4,128,128]{3,0,2,1:T(4,128)S(1)} %get-tuple-element.8), channel_id=1, source_target_pairs={{0,4},{4,8},{8,12},{12,16},{16,20},{20,24},{24,28},{1,5},{5,9},{9,... | collective-permute-start | bytes 3145736 | tf_op jit(solution)/shard_map/ppermute | solution.py:12
Sparse Core Ops, SparseCore 0:
  8.9 37.2 all-gather.2
  219.2 25.2 reduce-scatter.1
where the time goes:
time: 252 us; the launch traced here: 251 us
  waiting for transfers between devices  122 us (48%)
  local copies, waits for them, and re-layouts  40.7 us (16%)
  matrix products  33.8 us (13%)
  starting transfers between devices  21.5 us (9%)
  between operations  14.3 us (6%)
  blocking collectives  11.7 us (5%)
  other arithmetic  7.63 us (3%)
    ppermute x8, waiting for transfers between devices, shifted(): lax.ppermute(value, axis, [(source, source + steps) for source in range(i...  85.9 us
    reduce_scatter x1, waiting for transfers between devices, per_device(): result = lax.psum_scatter(mine, 'grp', scatter_dimension=0, tiled=True)  25.4 us
    ppermute x8, starting transfers between devices, shifted(): lax.ppermute(value, axis, [(source, source + steps) for source in range(i...  21.5 us
    gather x2, local copies, waits for them, and re-layouts, per_device(): near_p = jnp.take(wide_p, local_near, axis=0)  15.2 us
    dot_general x1, matrix products, per_device(): products = jnp.einsum('ekab,ekjbc->ekjac', a_blocks, near_p, precision=HIGH)  11.4 us
    dot_general x1, matrix products, per_device(): summed = jnp.einsum('ejskl,eklac->ejsac', select, products, precision=HIGH)  9.94 us
    all_gather x1, waiting for transfers between devices, per_device(): lax.all_gather(p_blocks, 'grp', axis=0, tiled=True)  9.61 us
    transpose x1, local copies, waits for them, and re-layouts, per_device(): products = jnp.einsum('ekab,ekjbc->ekjac', a_blocks, near_p, precision=HIGH)  8.87 us
  transfers between devices with their start and end apart: 10, of which 5 were waited for; matrix products, arithmetic and copies ran while one was open for 4% of the time, Pallas kernels for 0%

commit v1 on v0

v1 whole, which is shorter than its diff:
```python
import functools

import jax
import jax.numpy as jnp
from jax import lax
from jax.experimental import pallas as pl
from jax.experimental.pallas import tpu as pltpu
from jax.sharding import PartitionSpec as P

UNROLL = 4


def split(value):
    high = value.astype(jnp.bfloat16)
    low = (value - high.astype(jnp.float32)).astype(jnp.bfloat16)
    return high, low


def left_kernel(a_ref, p_ref, q_ref):
    slots, size = p_ref.shape[1], p_ref.shape[2]
    rows = []
    for j in range(slots):
        high, low = split(p_ref[0, j].T)
        rows.append(jnp.concatenate([high, high, low], axis=1))
    left = jnp.concatenate(rows, axis=0)
    for k in range(a_ref.shape[1]):
        high, low = split(a_ref[0, k])
        right = jnp.concatenate([high, low, high], axis=0)
        product = jnp.dot(left, right, preferred_element_type=jnp.float32)
        for j in range(slots):
            q_ref[0, j, k] = product[j * size : (j + 1) * size]


def left_products(a_blocks, p_blocks):
    count, near, size, _ = a_blocks.shape
    slots = p_blocks.shape[1]
    return pl.pallas_call(
        left_kernel,
        grid=(count,),
        in_specs=[
            pl.BlockSpec((1, near, size, size), lambda e: (e, 0, 0, 0)),
            pl.BlockSpec((1, slots, size, size), lambda e: (e, 0, 0, 0)),
        ],
        out_specs=pl.BlockSpec((1, slots, near, size, size), lambda e: (e, 0, 0, 0, 0)),
        out_shape=jax.ShapeDtypeStruct((count, slots, near, size, size), jnp.float32),
        compiler_params=pltpu.CompilerParams(vmem_limit_bytes=32 * 1024 * 1024),
        cost_estimate=pl.CostEstimate(
            flops=2 * 3 * count * near * slots * size**3,
            bytes_accessed=4 * size * size * count * (near + slots + near * slots),
            transcendentals=0,
        ),
        name="left_products",
    )(a_blocks, p_blocks)


def bits(count):
    return max(1, (count - 1).bit_length())


def list_kernel(
    sizes, place, near_ref, near_count, cols, col_count, slot_of, pattern, mine, theirs, list_ref, total_ref
):
    e_local, n_slot, p_slot, pat, groups, agg_slab = sizes
    blocks = e_local * p_slot
    p_bits, o_bits = bits(8 * blocks), bits(12 * (agg_slab // groups) * pat + 1)
    row, grp = place[0], place[1]
    core = lax.bitwise_and(grp, 1)
    edge = jnp.logical_or(grp == 0, grp == groups - 1)
    per_owner = agg_slab // groups

    def over_e(e, found):
        def over_k(k, found):
            n = near_ref[e, k]
            home = n // e_local
            inner = n - home * e_local
            home_row = home // groups
            offset = home_row - row
            crossed = lax.bitwise_xor(home - home_row * groups, grp)
            in_slab = offset == 0
            rim_theirs = jnp.where(offset < 0, 1 - core, core)
            part = jnp.where(in_slab, lax.shift_right_logical(crossed, 1), 2)
            other = jnp.where(in_slab, lax.bitwise_and(crossed, 1), rim_theirs)
            rim_buffer = jnp.where(
                rim_theirs == 0, jnp.where(edge, 4, 5), jnp.where(edge, 7, 6)
            )
            buffer = jnp.where(in_slab, crossed, rim_buffer)

            def over_l(l, found):
                at = inner * p_slot + l
                d = jnp.where(other == 0, mine[part, at], theirs[part, at])

                def over_j(j, found):
                    c = cols[e, j]
                    slab_at = c // agg_slab - row + 1
                    owner = lax.bitwise_xor(slot_of[c] // per_owner, grp)
                    inner_slot = lax.rem(slot_of[c], per_owner)
                    half = lax.bitwise_and(owner, 1)
                    upper = lax.shift_right_logical(owner, 1)
                    out = ((half * 2 + upper) * 3 + slab_at) * per_owner + inner_slot
                    q = (e * p_slot + j) * n_slot + k
                    code = ((q << p_bits) + (buffer * blocks + at) << o_bits) + out * pat
                    for s in range(pat):
                        list_ref[found] = code + s
                        found = found + (pattern[c, s] == d).astype(jnp.int32)
                    return found

                return lax.fori_loop(0, jnp.where(d >= 0, col_count[e], 0), over_j, found)

            return lax.fori_loop(0, p_slot, over_l, found)

        return lax.fori_loop(0, near_count[e], over_k, found)

    found = lax.fori_loop(0, e_local, over_e, jnp.int32(0))
    total_ref[0] = found
    for pad in range(UNROLL):
        list_ref[found + pad] = 12 * per_owner * pat


def tuple_list(place, neighbours, neighbour_count, p_columns, p_count, coarse_slot, pattern, mine, theirs, groups, agg_slab):
    e_local, n_slot = neighbours.shape
    p_slot, pat = p_columns.shape[1], pattern.shape[1]
    sizes = (e_local, n_slot, p_slot, pat, groups, agg_slab)
    longest = e_local * n_slot * p_slot * p_slot * pat + UNROLL
    smem = pl.BlockSpec(memory_space=pltpu.SMEM)
    return pl.pallas_call(
        functools.partial(list_kernel, sizes),
        in_specs=[smem] * 9,
        out_specs=[smem] * 2,
        out_shape=[jax.ShapeDtypeStruct((longest,), jnp.int32), jax.ShapeDtypeStruct((1,), jnp.int32)],
        cost_estimate=pl.CostEstimate(flops=4000000, bytes_accessed=4000000, transcendentals=0),
        name="tuple_list",
    )(place, neighbours, neighbour_count, p_columns, p_count, coarse_slot, pattern, mine, theirs)


def sum_kernel(sizes, list_ref, total_ref, q_ref, *refs):
    blocks, kept = sizes
    p_refs, (keep, send, acc, q_buf, p_buf, sems, out_sems) = refs[:8], refs[8:]
    p_bits, o_bits = bits(8 * blocks), bits(2 * kept + 1)
    size = q_ref.shape[-1]

    def fetch(chunk, slot):
        for u in range(UNROLL):
            code = lax.shift_right_logical(list_ref[chunk * UNROLL + u], o_bits)
            q = lax.shift_right_logical(code, p_bits)
            at = lax.bitwise_and(code, (1 << p_bits) - 1)
            buffer = at // blocks
            inner = at - buffer * blocks
            pltpu.make_async_copy(q_ref.at[q], q_buf.at[slot, u], sems.at[slot, u, 0]).start()
            for b in range(8):

                @pl.when(buffer == b)
                def _():
                    pltpu.make_async_copy(
                        p_refs[b].at[inner], p_buf.at[slot, u], sems.at[slot, u, 1]
                    ).start()

    chunks = (total_ref[0] + UNROLL - 1) // UNROLL

    @pl.when(chunks > 0)
    def _():
        fetch(0, 0)

    def clear(i, carry):
        acc[i] = jnp.zeros((size, size), jnp.float32)
        return carry

    lax.fori_loop(0, 2 * kept + 1, clear, 0)

    def step(chunk, carry):
        slot = lax.rem(chunk, 2)

        @pl.when(chunk + 1 < chunks)
        def _():
            fetch(chunk + 1, 1 - slot)

        products = []
        for u in range(UNROLL):
            pltpu.make_async_copy(q_ref.at[0], q_buf.at[slot, u], sems.at[slot, u, 0]).wait()
            pltpu.make_async_copy(p_refs[0].at[0], p_buf.at[slot, u], sems.at[slot, u, 1]).wait()
        for u in range(UNROLL):
            q_high, q_low = split(q_buf[slot, u])
            p_high, p_low = split(p_buf[slot, u])
            left = jnp.concatenate([q_high, q_high, q_low], axis=1)
            right = jnp.concatenate([p_high, p_low, p_high], axis=0)
            products.append(jnp.dot(left, right, preferred_element_type=jnp.float32))
        for u in range(UNROLL):
            out = lax.bitwise_and(list_ref[chunk * UNROLL + u], (1 << o_bits) - 1)
            acc[out] += products[u]
        return carry

    lax.fori_loop(0, chunks, step, 0)
    first = pltpu.make_async_copy(acc.at[pl.ds(kept, kept)], send, out_sems.at[0])
    second = pltpu.make_async_copy(acc.at[pl.ds(0, kept)], keep, out_sems.at[1])
    first.start()
    second.start()
    first.wait()
    second.wait()


def tuple_sums(entries, total, q_blocks, p_buffers, kept):
    size = q_blocks.shape[-1]
    blocks = p_buffers[0].shape[0]
    smem = pl.BlockSpec(memory_space=pltpu.SMEM)
    anywhere = pl.BlockSpec(memory_space=pl.ANY)
    return pl.pallas_call(
        functools.partial(sum_kernel, (blocks, kept)),
        in_specs=[smem, smem] + [anywhere] * 9,
        out_specs=[anywhere] * 2,
        out_shape=[jax.ShapeDtypeStruct((kept, size, size), jnp.float32)] * 2,
        scratch_shapes=[
            pltpu.VMEM((2 * kept + 1, size, size), jnp.float32),
            pltpu.VMEM((2, UNROLL, size, size), jnp.float32),
            pltpu.VMEM((2, UNROLL, size, size), jnp.float32),
            pltpu.SemaphoreType.DMA((2, UNROLL, 2)),
            pltpu.SemaphoreType.DMA((2,)),
        ],
        compiler_params=pltpu.CompilerParams(vmem_limit_bytes=32 * 1024 * 1024),
        cost_estimate=pl.CostEstimate(flops=10**9, bytes_accessed=10**7, transcendentals=0),
        name="tuple_sums",
    )(entries, total, q_blocks, *p_buffers)


def per_device(
    a_blocks, neighbours, neighbour_count, p_blocks, p_columns, p_count, coarse_slot, coarse_pattern
):
    rows, groups = lax.axis_size("rows"), lax.axis_size("grp")
    e_local, n_slot, size = a_blocks.shape[:3]
    p_slot = p_blocks.shape[1]
    pat = coarse_pattern.shape[1]
    agg_slab = coarse_slot.shape[0] // rows
    row, grp = lax.axis_index("rows"), lax.axis_index("grp")
    upper = groups // 2
    core_pairs = [(g, g ^ 1) for g in range(groups)]
    upper_pairs = [(g, g ^ upper) for g in range(groups)]

    def along(g, step):
        return [
            (r * groups + g, (r + step) * groups + g)
            for r in range(rows)
            if 0 <= r + step < rows
        ]

    first, last = 0, groups - 1
    direct = along(last, 1) + along(first, -1)
    forwarded = along(last ^ upper, 1) + along(first ^ upper, -1)
    both = ("rows", "grp")

    live = jnp.arange(p_slot, dtype=jnp.int32)[None, :] < p_count[:, None]
    own_cols = jnp.where(live, p_columns, -1).reshape(e_local * p_slot)
    across_cols = lax.ppermute(own_cols, "grp", upper_pairs)
    is_edge = (grp == first) | (grp == last)
    rim_cols = lax.ppermute(jnp.where(is_edge, own_cols, across_cols), both, direct + forwarded)
    mine = jnp.stack([own_cols, across_cols, rim_cols])
    theirs = lax.ppermute(mine, "grp", core_pairs)

    own = p_blocks.reshape(e_local * p_slot, size, size)
    across = lax.ppermute(own, "grp", upper_pairs)
    rim = lax.ppermute(own, both, direct)
    own_core = lax.ppermute(own, "grp", core_pairs)
    rim_core = lax.ppermute(rim, "grp", [(first, first ^ 1), (last, last ^ 1)])
    rim_far = lax.ppermute(across, both, forwarded)
    across_core = lax.ppermute(across, "grp", core_pairs)
    rim_far_core = lax.ppermute(
        rim_far, "grp", [(first ^ upper, first ^ upper ^ 1), (last ^ upper, last ^ upper ^ 1)]
    )

    place = jnp.stack([row, grp]).astype(jnp.int32)
    entries, total = tuple_list(
        place, neighbours, neighbour_count, p_columns, p_count, coarse_slot, coarse_pattern, mine, theirs, groups, agg_slab
    )
    q_blocks = left_products(a_blocks, p_blocks).reshape(e_local * p_slot * n_slot, size, size)
    per_owner = agg_slab // groups
    kept = 2 * 3 * per_owner * pat
    keep, send = tuple_sums(
        entries,
        total,
        q_blocks,
        [own, own_core, across, across_core, rim, rim_far, rim_core, rim_far_core],
        kept,
    )
    shape = (2, 3, per_owner, pat, size, size)
    chip = keep.reshape(shape) + lax.ppermute(send, "grp", core_pairs).reshape(shape)
    down, here, up = (
        chip[0, t] + lax.ppermute(chip[1, t], "grp", upper_pairs) for t in range(3)
    )
    from_next = lax.ppermute(down, "rows", [(r, r - 1) for r in range(1, rows)])
    from_prev = lax.ppermute(up, "rows", [(r, r + 1) for r in range(rows - 1)])
    return here + from_next + from_prev


def solution(mesh):
    return jax.shard_map(
        per_device,
        mesh=mesh,
        in_specs=(
            P(("rows", "grp"), None, None, None),
            P(("rows", "grp"), None),
            P(("rows", "grp")),
            P(("rows", "grp"), None, None, None),
            P(("rows", "grp"), None),
            P(("rows", "grp")),
            P(),
            P(),
        ),
        out_specs=P(("rows", "grp"), None, None, None),
        check_vma=False,
    )
```

time: 252 us -> 128 us (0.51)
  waiting for transfers between devices: 122 us -> 48.6 us
  matrix products: 33.8 us -> 0 us
  local copies, waits for them, and re-layouts: 40.7 us -> 12.2 us
  Pallas kernels: 0 us -> 28.1 us
  between operations: 14.3 us -> 0.21 us
  starting transfers between devices: 21.5 us -> 34.5 us
  blocking collectives: 11.7 us -> 0 us
  other arithmetic: 7.63 us -> 2.4 us
    ppermute x8 -> x16, waiting for transfers between devices: 85.9 us -> 48.6 us  [the longest x1 22.1 us: per_device(): across = lax.ppermute(own, 'grp', upper_pairs)]
    dot_general x4 -> x0, matrix products: 33.8 us -> none  [the longest x1 11.4 us: per_device(): products = jnp.einsum('ekab,ekjbc->ekjac', a_blocks, near_p, precision=HIGH)]
    pallas_call x0 -> x3, Pallas kernels: none -> 28.1 us  [the longest x1 16.8 us: tuple_sums(): pl.pallas_call(functools.partial(sum_kernel, (blocks, kept)), in_specs=[s...]
    reduce_scatter x1 -> x0, waiting for transfers between devices: 25.4 us -> none  [per_device(): result = lax.psum_scatter(mine, 'grp', scatter_dimension=0, tiled=True)]
    gather x10 -> x0, local copies, waits for them, and re-layouts: 18.1 us -> none  [the longest x2 15.2 us: per_device(): near_p = jnp.take(wide_p, local_near, axis=0)]
    transpose x2 -> x0, local copies, waits for them, and re-layouts: 14.4 us -> none  [the longest x1 8.87 us: per_device(): products = jnp.einsum('ekab,ekjbc->ekjac', a_blocks, near_p, precision=HIGH)]
    ppermute x8 -> x16, starting transfers between devices: 21.5 us -> 34.5 us  [the longest x1 12.8 us: per_device(): across_cols = lax.ppermute(own_cols, 'grp', upper_pairs)]
    all_gather x1 -> x0, waiting for transfers between devices: 9.61 us -> none  [per_device(): lax.all_gather(p_blocks, 'grp', axis=0, tiled=True)]
  transfers between devices with their start and end apart: 10 -> 16, of which waited for: 5 -> 7; matrix products, arithmetic and copies ran while one was open for 4% -> 2% of each run, Pallas kernels for 0% -> 9%
where the time goes in v1:
time: 128 us; the launch traced here: 126 us
  waiting for transfers between devices  48.6 us (38%)
  starting transfers between devices  34.5 us (27%)
  Pallas kernels  28.1 us (22%)
  local copies, waits for them, and re-layouts  12.2 us (10%)
  other arithmetic  2.4 us (2%)
    ppermute x1, waiting for transfers between devices, per_device(): across = lax.ppermute(own, 'grp', upper_pairs)  22.1 us
    pallas_call x1, Pallas kernels, tuple_sums(): pl.pallas_call(functools.partial(sum_kernel, (blocks, kept)), in_specs=[s...  16.8 us
    ppermute x1, starting transfers between devices, per_device(): across_cols = lax.ppermute(own_cols, 'grp', upper_pairs)  12.8 us
    ppermute x3, waiting for transfers between devices, per_device(): lax.ppermute(chip[1, t], 'grp', upper_pairs)  12.7 us
    unnamed x22, local copies, waits for them, and re-layouts  11.9 us
    pallas_call x1, Pallas kernels, tuple_list(): pl.pallas_call(functools.partial(list_kernel, sizes), in_specs=[smem] * 9...  6.69 us
    pallas_call x1, Pallas kernels, left_products(): pl.pallas_call(left_kernel, grid=(count,), in_specs=[pl.BlockSpec((1, nea...  4.66 us
    ppermute x1, starting transfers between devices, per_device(): from_prev = lax.ppermute(up, 'rows', [(r, r + 1) for r in range(rows - 1)])  4.56 us
  transfers between devices with their start and end apart: 16, of which 7 were waited for; matrix products, arithmetic and copies ran while one was open for 2% of the time, Pallas kernels for 9%

profile of v1, /device:TPU:0, one launch (start us, length us, event | category | flops | bytes accessed | tf_op | source)
XLA Modules:
  0.0 126.1 jit_solution(4290455300369845245)
XLA Ops:
  0.0 3.0 %collective-permute-start.4 = (f32[16,128,128]{2,1,0:T(8,128)}, f32[16,128,128]{2,1,0:T(8,128)S(1)}, u32[]{:S(2)}, u32[]{:S(2)}) collective-permute-start(f32[16,128,128]{2,1,0:T(8,128)} %bitcast.32), channel_id=1, source_target_pairs={{0,2},{1,3},{2,0},{3,1},{4,6},{5,7},{6,4},{7,5},{8,10},{9,11},{10,... | collective-permute-start | bytes 3145736 | tf_op jit(solution)/shard_map/ppermute | solution.py:257
  3.0 1.3 %collective-permute-start.6 = (f32[16,128,128]{2,1,0:T(8,128)}, f32[16,128,128]{2,1,0:T(8,128)S(1)}, u32[]{:S(2)}, u32[]{:S(2)}) collective-permute-start(f32[16,128,128]{2,1,0:T(8,128)} %bitcast.33), channel_id=1, source_target_pairs={{3,7},{7,11},{11,15},{15,19},{19,23},{23,27},{27,31},{4,0},{8,4},{... | collective-permute-start | bytes 3145736 | tf_op jit(solution)/shard_map/ppermute | solution.py:258
  4.3 22.1 %collective-permute-done.4.refs_2_ = f32[16,128,128]{2,1,0:T(8,128)S(1)} collective-permute-done((f32[16,128,128]{2,1,0:T(8,128)}, f32[16,128,128]{2,1,0:T(8,128)S(1)}, u32[]{:S(2)}, u32[]{:S(2)}) %collective-permute-start.4) | collective-permute-done | bytes 1048608 | tf_op jit(solution)/shard_map/ppermute | solution.py:257
  26.3 1.7 %collective-permute-start.7 = (f32[16,128,128]{2,1,0:T(8,128)S(1)}, f32[16,128,128]{2,1,0:T(8,128)}, u32[]{:S(2)}, u32[]{:S(2)}) collective-permute-start(f32[16,128,128]{2,1,0:T(8,128)S(1)} %collective-permute-done.4.refs_2_), channel_id=1, source_target_pairs={{1,5},{5,9},{9,13},{13,17},{17,21},{21,25},{25,29},{6,2},{10,6},{1... | collective-permute-start | bytes 3145736 | tf_op jit(solution)/shard_map/ppermute | solution.py:261
  28.0 1.6 %collective-permute-start.3 = (f32[16,128,128]{2,1,0:T(8,128)}, f32[16,128,128]{2,1,0:T(8,128)}, u32[]{:S(2)}, u32[]{:S(2)}) collective-permute-start(f32[16,128,128]{2,1,0:T(8,128)} %bitcast.34), channel_id=1, source_target_pairs={{0,1},{1,0},{2,3},{3,2},{4,5},{5,4},{6,7},{7,6},{8,9},{9,8},{10,11... | collective-permute-start | bytes 3145736 | tf_op jit(solution)/shard_map/ppermute | solution.py:259
  29.6 3.4 %collective-permute-start.8 = (f32[16,128,128]{2,1,0:T(8,128)S(1)}, f32[16,128,128]{2,1,0:T(8,128)}, u32[]{:S(2)}, u32[]{:S(2)}) collective-permute-start(f32[16,128,128]{2,1,0:T(8,128)S(1)} %collective-permute-done.6.refs_4_), channel_id=1, source_target_pairs={{0,1},{3,2},{4,5},{7,6},{8,9},{11,10},{12,13},{15,14},{16,17},{19,... | collective-permute-start | bytes 3145736 | tf_op jit(solution)/shard_map/ppermute | solution.py:260
  33.0 1.3 %collective-permute-start.9 = (f32[16,128,128]{2,1,0:T(8,128)}, f32[16,128,128]{2,1,0:T(8,128)}, u32[]{:S(2)}, u32[]{:S(2)}) collective-permute-start(f32[16,128,128]{2,1,0:T(8,128)} %collective-permute-done.7.refs_5_), channel_id=1, source_target_pairs={{2,3},{1,0},{6,7},{5,4},{10,11},{9,8},{14,15},{13,12},{18,19},{17,... | collective-permute-start | bytes 3145736 | tf_op jit(solution)/shard_map/ppermute | solution.py:263
  35.2 12.8 %collective-permute-start = (s32[16]{0:T(128)S(1)}, s32[16]{0:T(128)S(1)}, u32[]{:S(2)}, u32[]{:S(2)}) collective-permute-start(s32[16]{0:T(128)S(1)} %reshape.33), channel_id=1, source_target_pairs={{0,2},{1,3},{2,0},{3,1},{4,6},{5,7},{6,4},{7,5},{8,10},{9,11},{10,... | collective-permute-start | bytes 200 | tf_op jit(solution)/shard_map/ppermute | solution.py:250
  49.9 2.0 %copy-done.4 = f32[8,7,128,128]{3,2,1,0:T(8,128)S(1)} copy-done((f32[8,7,128,128]{3,2,1,0:T(8,128)S(1)}, f32[8,7,128,128]{3,2,1,0:T(8,128)}, u32[]{:S(2)}) %copy-start.4) | copy-done | bytes 3670040
  51.9 4.7 %left_products.1 = f32[8,2,7,128,128]{4,3,2,1,0:T(8,128)S(1)} custom-call(f32[8,7,128,128]{3,2,1,0:T(8,128)S(1)} %copy-done.4, f32[8,2,128,128]{3,2,1,0:T(8,128)S(1)} %copy-done.2), custom_call_target="tpu_custom_call" | custom-call | flops 1409286144 | bytes 12058624 | tf_op jit(solution)/shard_map/left_products/pallas_call | solution.py:37
  56.6 2.9 %copy-done = f32[8,2,7,128,128]{4,3,2,1,0:T(8,128)} copy-done((f32[8,2,7,128,128]{4,3,2,1,0:T(8,128)}, f32[8,2,7,128,128]{4,3,2,1,0:T(8,128)S(1)}, u32[]{:S(2)}) %copy-start) | copy-done | bytes 7340056
  59.5 1.3 %collective-permute-start.1 = (s32[16]{0:T(128)S(1)}, s32[16]{0:T(128)S(1)}, u32[]{:S(2)}, u32[]{:S(2)}) collective-permute-start(s32[16]{0:T(128)S(1)} %broadcast_select_fusion), channel_id=1, source_target_pairs={{3,7},{7,11},{11,15},{15,19},{19,23},{23,27},{27,31},{4,0},{8,4},{... | collective-permute-start | bytes 200 | tf_op jit(solution)/shard_map/ppermute | solution.py:252
  60.9 4.4 %collective-permute-done.1 = s32[16]{0:T(128)S(1)} collective-permute-done((s32[16]{0:T(128)S(1)}, s32[16]{0:T(128)S(1)}, u32[]{:S(2)}, u32[]{:S(2)}) %collective-permute-start.1) | collective-permute-done | bytes 96 | tf_op jit(solution)/shard_map/ppermute | solution.py:252
  67.4 6.7 %tuple_list.1 = (s32[900]{0:T(1024)}, s32[1]{0:T(128)}) custom-call(s32[2]{0:T(128)} %pad_add_fusion.1.place, s32[8,7]{1,0:T(8,128)} %near_ref.1, s32[8]{0:T(128)} %near_count.1, s32[8,2]{1,0:T(8,128)} %copy.21.cols, s32[8]{0:T(128)} %col_count.1, s32[32]{0:T(128)} %slot_of.1, s32[32,4]{1,0:T(8,128)} %copy.22.pattern, s32[3,16]{1,0:T(4,128)} %copy-done.6, ...), custom_call_target="tpu_custom_call" | custom-call | flops 4000000 | bytes 4000000 | tf_op jit(solution)/shard_map/tuple_list/pallas_call | solution.py:125
  74.2 3.1 %copy-done.1 = f32[8,2,7,128,128]{4,3,2,1,0:T(8,128)S(1)} copy-done((f32[8,2,7,128,128]{4,3,2,1,0:T(8,128)S(1)}, f32[8,2,7,128,128]{4,3,2,1,0:T(8,128)}, u32[]{:S(2)}) %copy-start.1) | copy-done | bytes 7340056
  77.9 16.8 %tuple_sums.1 = (f32[24,128,128]{2,1,0:T(8,128)S(1)}, f32[24,128,128]{2,1,0:T(8,128)S(1)}) custom-call(s32[900]{0:T(1024)S(1)} %copy-done.5, s32[1]{0:T(128)} %get-tuple-element.10.total_ref, f32[112,128,128]{2,1,0:T(8,128)S(1)} %bitcast.31, f32[16,128,128]{2,1,0:T(8,128)S(1)} %bitcast.35, f32[16,128,128]{2,1,0:T(8,128)} %collective-permute-done.3.refs_1_, ...), custom_call_target="tpu_custom_call" | custom-call | flops 1000000000 | bytes 10000000 | tf_op jit(solution)/shard_map/tuple_sums/pallas_call | solution.py:205
  94.8 3.4 %collective-permute-done.10 = f32[24,128,128]{2,1,0:T(8,128)S(1)} collective-permute-done((f32[24,128,128]{2,1,0:T(8,128)S(1)}, f32[24,128,128]{2,1,0:T(8,128)S(1)}, u32[]{:S(2)}, u32[]{:S(2)}) %collective-permute-start.10) | collective-permute-done | bytes 1572896 | tf_op jit(solution)/shard_map/ppermute | solution.py:282
  98.6 2.0 %collective-permute-start.12 = (f32[1,4,128,128]{3,2,1,0:T(8,128)S(1)}, f32[1,4,128,128]{3,2,1,0:T(8,128)S(1)}, u32[]{:S(2)}, u32[]{:S(2)}) collective-permute-start(f32[1,4,128,128]{3,2,1,0:T(8,128)S(1)} %get-tuple-element.15), channel_id=1, source_target_pairs={{0,2},{1,3},{2,0},{3,1},{4,6},{5,7},{6,4},{7,5},{8,10},{9,11},{10,... | collective-permute-start | bytes 786440 | tf_op jit(solution)/shard_map/ppermute | solution.py:284
  100.7 7.0 %collective-permute-done.14 = f32[1,4,128,128]{3,2,1,0:T(8,128)S(1)} collective-permute-done((f32[1,4,128,128]{3,2,1,0:T(8,128)S(1)}, f32[1,4,128,128]{3,2,1,0:T(8,128)S(1)}, u32[]{:S(2)}, u32[]{:S(2)}) %collective-permute-start.14) | collective-permute-done | bytes 262176 | tf_op jit(solution)/shard_map/ppermute | solution.py:284
  107.7 5.6 %collective-permute-done.12 = f32[1,4,128,128]{3,2,1,0:T(8,128)S(1)} collective-permute-done((f32[1,4,128,128]{3,2,1,0:T(8,128)S(1)}, f32[1,4,128,128]{3,2,1,0:T(8,128)S(1)}, u32[]{:S(2)}, u32[]{:S(2)}) %collective-permute-start.12) | collective-permute-done | bytes 262176 | tf_op jit(solution)/shard_map/ppermute | solution.py:284
  113.4 1.3 %collective-permute-start.13 = (f32[1,4,128,128]{3,2,1,0:T(8,128)S(1)}, f32[1,4,128,128]{3,2,1,0:T(8,128)S(1)}, u32[]{:S(2)}, u32[]{:S(2)}) collective-permute-start(f32[1,4,128,128]{3,2,1,0:T(8,128)S(1)} %get-tuple-element.16), channel_id=1, source_target_pairs={{4,0},{8,4},{12,8},{16,12},{20,16},{24,20},{28,24},{5,1},{9,5},{13... | collective-permute-start | bytes 786440 | tf_op jit(solution)/shard_map/ppermute | solution.py:286
  114.7 4.6 %collective-permute-start.15 = (f32[1,4,128,128]{3,2,1,0:T(8,128)S(1)}, f32[1,4,128,128]{3,2,1,0:T(8,128)S(1)}, u32[]{:S(2)}, u32[]{:S(2)}) collective-permute-start(f32[1,4,128,128]{3,2,1,0:T(8,128)S(1)} %get-tuple-element.17), channel_id=1, source_target_pairs={{0,4},{4,8},{8,12},{12,16},{16,20},{20,24},{24,28},{1,5},{5,9},{9,... | collective-permute-start | bytes 786440 | tf_op jit(solution)/shard_map/ppermute | solution.py:287
  119.3 2.7 %collective-permute-done.13 = f32[1,4,128,128]{3,2,1,0:T(8,128)S(1)} collective-permute-done((f32[1,4,128,128]{3,2,1,0:T(8,128)S(1)}, f32[1,4,128,128]{3,2,1,0:T(8,128)S(1)}, u32[]{:S(2)}, u32[]{:S(2)}) %collective-permute-start.13) | collective-permute-done | bytes 262176 | tf_op jit(solution)/shard_map/ppermute | solution.py:286
  122.0 3.3 %collective-permute-done.15 = f32[1,4,128,128]{3,2,1,0:T(8,128)S(1)} collective-permute-done((f32[1,4,128,128]{3,2,1,0:T(8,128)S(1)}, f32[1,4,128,128]{3,2,1,0:T(8,128)S(1)}, u32[]{:S(2)}, u32[]{:S(2)}) %collective-permute-start.15) | collective-permute-done | bytes 262176 | tf_op jit(solution)/shard_map/ppermute | solution.py:287
  (44 shorter events, 6.9 us)
Async XLA Ops:
  0.0 26.3 %collective-permute-start.4 = (f32[16,128,128]{2,1,0:T(8,128)}, f32[16,128,128]{2,1,0:T(8,128)S(1)}, u32[]{:S(2)}, u32[]{:S(2)}) collective-permute-start(f32[16,128,128]{2,1,0:T(8,128)} %bitcast.32), channel_id=1, source_target_pairs={{0,2},{1,3},{2,0},{3,1},{4,6},{5,7},{6,4},{7,5},{8,10},{9,11},{10,... | collective-permute-start | bytes 3145736 | tf_op jit(solution)/shard_map/ppermute | solution.py:257
  3.0 26.7 %collective-permute-start.6 = (f32[16,128,128]{2,1,0:T(8,128)}, f32[16,128,128]{2,1,0:T(8,128)S(1)}, u32[]{:S(2)}, u32[]{:S(2)}) collective-permute-start(f32[16,128,128]{2,1,0:T(8,128)} %bitcast.33), channel_id=1, source_target_pairs={{3,7},{7,11},{11,15},{15,19},{19,23},{23,27},{27,31},{4,0},{8,4},{... | collective-permute-start | bytes 3145736 | tf_op jit(solution)/shard_map/ppermute | solution.py:258
  26.3 6.7 %collective-permute-start.7 = (f32[16,128,128]{2,1,0:T(8,128)S(1)}, f32[16,128,128]{2,1,0:T(8,128)}, u32[]{:S(2)}, u32[]{:S(2)}) collective-permute-start(f32[16,128,128]{2,1,0:T(8,128)S(1)} %collective-permute-done.4.refs_2_), channel_id=1, source_target_pairs={{1,5},{5,9},{9,13},{13,17},{17,21},{21,25},{25,29},{6,2},{10,6},{1... | collective-permute-start | bytes 3145736 | tf_op jit(solution)/shard_map/ppermute | solution.py:261
  28.0 46.1 %collective-permute-start.3 = (f32[16,128,128]{2,1,0:T(8,128)}, f32[16,128,128]{2,1,0:T(8,128)}, u32[]{:S(2)}, u32[]{:S(2)}) collective-permute-start(f32[16,128,128]{2,1,0:T(8,128)} %bitcast.34), channel_id=1, source_target_pairs={{0,1},{1,0},{2,3},{3,2},{4,5},{5,4},{6,7},{7,6},{8,9},{9,8},{10,11... | collective-permute-start | bytes 3145736 | tf_op jit(solution)/shard_map/ppermute | solution.py:259
  29.6 44.5 %collective-permute-start.5 = (f32[16,128,128]{2,1,0:T(8,128)S(1)}, f32[16,128,128]{2,1,0:T(8,128)}, u32[]{:S(2)}, u32[]{:S(2)}) collective-permute-start(f32[16,128,128]{2,1,0:T(8,128)S(1)} %collective-permute-done.4.refs_2_), channel_id=1, source_target_pairs={{0,1},{1,0},{2,3},{3,2},{4,5},{5,4},{6,7},{7,6},{8,9},{9,8},{10,11... | collective-permute-start | bytes 3145736 | tf_op jit(solution)/shard_map/ppermute | solution.py:262
  29.6 44.5 %collective-permute-start.8 = (f32[16,128,128]{2,1,0:T(8,128)S(1)}, f32[16,128,128]{2,1,0:T(8,128)}, u32[]{:S(2)}, u32[]{:S(2)}) collective-permute-start(f32[16,128,128]{2,1,0:T(8,128)S(1)} %collective-permute-done.6.refs_4_), channel_id=1, source_target_pairs={{0,1},{3,2},{4,5},{7,6},{8,9},{11,10},{12,13},{15,14},{16,17},{19,... | collective-permute-start | bytes 3145736 | tf_op jit(solution)/shard_map/ppermute | solution.py:260
  33.0 41.1 %collective-permute-start.9 = (f32[16,128,128]{2,1,0:T(8,128)}, f32[16,128,128]{2,1,0:T(8,128)}, u32[]{:S(2)}, u32[]{:S(2)}) collective-permute-start(f32[16,128,128]{2,1,0:T(8,128)} %collective-permute-done.7.refs_5_), channel_id=1, source_target_pairs={{2,3},{1,0},{6,7},{5,4},{10,11},{9,8},{14,15},{13,12},{18,19},{17,... | collective-permute-start | bytes 3145736 | tf_op jit(solution)/shard_map/ppermute | solution.py:263
  35.2 24.4 %collective-permute-start = (s32[16]{0:T(128)S(1)}, s32[16]{0:T(128)S(1)}, u32[]{:S(2)}, u32[]{:S(2)}) collective-permute-start(s32[16]{0:T(128)S(1)} %reshape.33), channel_id=1, source_target_pairs={{0,2},{1,3},{2,0},{3,1},{4,6},{5,7},{6,4},{7,5},{8,10},{9,11},{10,... | collective-permute-start | bytes 200 | tf_op jit(solution)/shard_map/ppermute | solution.py:250
  48.6 1.2 copy-start.2
  49.9 2.0 %copy-start.4 = (f32[8,7,128,128]{3,2,1,0:T(8,128)S(1)}, f32[8,7,128,128]{3,2,1,0:T(8,128)}, u32[]{:S(2)}) copy-start(f32[8,7,128,128]{3,2,1,0:T(8,128)} %a_ref.1) | copy-start | bytes 11010052
  51.9 13.5 %copy-start.7 = (s32[8,2]{0,1:T(2,128)S(1)}, s32[8,2]{0,1:T(2,128)}, u32[]{:S(2)}) copy-start(s32[8,2]{0,1:T(2,128)} %param.12) | copy-start | bytes 196
  51.9 14.2 %copy-start.8 = (s32[32,4]{0,1:T(4,128)S(1)}, s32[32,4]{0,1:T(4,128)}, u32[]{:S(2)}) copy-start(s32[32,4]{0,1:T(4,128)} %param.15) | copy-start | bytes 1540
  51.9 22.2 %copy-start.3 = (f32[8,2,128,128]{3,2,1,0:T(8,128)S(1)}, f32[8,2,128,128]{3,2,1,0:T(8,128)}, u32[]{:S(2)}) copy-start(f32[8,2,128,128]{3,2,1,0:T(8,128)} %p_ref.1) | copy-start | bytes 3145732
  56.6 2.9 %copy-start = (f32[8,2,7,128,128]{4,3,2,1,0:T(8,128)}, f32[8,2,7,128,128]{4,3,2,1,0:T(8,128)S(1)}, u32[]{:S(2)}) copy-start(f32[8,2,7,128,128]{4,3,2,1,0:T(8,128)S(1)} %left_products.1) | copy-start | bytes 22020100
  59.5 5.8 %collective-permute-start.1 = (s32[16]{0:T(128)S(1)}, s32[16]{0:T(128)S(1)}, u32[]{:S(2)}, u32[]{:S(2)}) collective-permute-start(s32[16]{0:T(128)S(1)} %broadcast_select_fusion), channel_id=1, source_target_pairs={{3,7},{7,11},{11,15},{15,19},{19,23},{23,27},{27,31},{4,0},{8,4},{... | collective-permute-start | bytes 200 | tf_op jit(solution)/shard_map/ppermute | solution.py:252
  65.3 1.5 %copy-start.6 = (s32[3,16]{1,0:T(4,128)}, s32[3,16]{1,0:T(4,128)S(1)}, u32[]{:S(2)}) copy-start(s32[3,16]{1,0:T(4,128)S(1)} %pad_add_fusion.mine) | copy-start | bytes 580
  65.3 1.5 %collective-permute-start.2 = (s32[3,16]{1,0:T(4,128)S(1)}, s32[3,16]{1,0:T(4,128)S(1)}, u32[]{:S(2)}, u32[]{:S(2)}) collective-permute-start(s32[3,16]{1,0:T(4,128)S(1)} %pad_add_fusion.mine), channel_id=1, source_target_pairs={{0,1},{1,0},{2,3},{3,2},{4,5},{5,4},{6,7},{7,6},{8,9},{9,8},{10,11... | collective-permute-start | bytes 584 | tf_op jit(solution)/shard_map/ppermute | solution.py:254
  74.2 3.1 %copy-start.1 = (f32[8,2,7,128,128]{4,3,2,1,0:T(8,128)S(1)}, f32[8,2,7,128,128]{4,3,2,1,0:T(8,128)}, u32[]{:S(2)}) copy-start(f32[8,2,7,128,128]{4,3,2,1,0:T(8,128)} %copy-done) | copy-start | bytes 22020100
  94.7 3.5 %collective-permute-start.10 = (f32[24,128,128]{2,1,0:T(8,128)S(1)}, f32[24,128,128]{2,1,0:T(8,128)S(1)}, u32[]{:S(2)}, u32[]{:S(2)}) collective-permute-start(f32[24,128,128]{2,1,0:T(8,128)S(1)} %get-tuple-element.12), channel_id=1, source_target_pairs={{0,1},{1,0},{2,3},{3,2},{4,5},{5,4},{6,7},{7,6},{8,9},{9,8},{10,11... | collective-permute-start | bytes 4718600 | tf_op jit(solution)/shard_map/ppermute | solution.py:282
  98.5 9.2 %collective-permute-start.14 = (f32[1,4,128,128]{3,2,1,0:T(8,128)S(1)}, f32[1,4,128,128]{3,2,1,0:T(8,128)S(1)}, u32[]{:S(2)}, u32[]{:S(2)}) collective-permute-start(f32[1,4,128,128]{3,2,1,0:T(8,128)S(1)} %get-tuple-element.14), channel_id=1, source_target_pairs={{0,2},{1,3},{2,0},{3,1},{4,6},{5,7},{6,4},{7,5},{8,10},{9,11},{10,... | collective-permute-start | bytes 786440 | tf_op jit(solution)/shard_map/ppermute | solution.py:284
  98.6 14.8 %collective-permute-start.12 = (f32[1,4,128,128]{3,2,1,0:T(8,128)S(1)}, f32[1,4,128,128]{3,2,1,0:T(8,128)S(1)}, u32[]{:S(2)}, u32[]{:S(2)}) collective-permute-start(f32[1,4,128,128]{3,2,1,0:T(8,128)S(1)} %get-tuple-element.15), channel_id=1, source_target_pairs={{0,2},{1,3},{2,0},{3,1},{4,6},{5,7},{6,4},{7,5},{8,10},{9,11},{10,... | collective-permute-start | bytes 786440 | tf_op jit(solution)/shard_map/ppermute | solution.py:284
  100.6 18.7 %collective-permute-start.11 = (f32[1,4,128,128]{3,2,1,0:T(8,128)S(1)}, f32[1,4,128,128]{3,2,1,0:T(8,128)S(1)}, u32[]{:S(2)}, u32[]{:S(2)}) collective-permute-start(f32[1,4,128,128]{3,2,1,0:T(8,128)S(1)} %get-tuple-element.13), channel_id=1, source_target_pairs={{0,2},{1,3},{2,0},{3,1},{4,6},{5,7},{6,4},{7,5},{8,10},{9,11},{10,... | collective-permute-start | bytes 786440 | tf_op jit(solution)/shard_map/ppermute | solution.py:284
  113.4 8.6 %collective-permute-start.13 = (f32[1,4,128,128]{3,2,1,0:T(8,128)S(1)}, f32[1,4,128,128]{3,2,1,0:T(8,128)S(1)}, u32[]{:S(2)}, u32[]{:S(2)}) collective-permute-start(f32[1,4,128,128]{3,2,1,0:T(8,128)S(1)} %get-tuple-element.16), channel_id=1, source_target_pairs={{4,0},{8,4},{12,8},{16,12},{20,16},{24,20},{28,24},{5,1},{9,5},{13... | collective-permute-start | bytes 786440 | tf_op jit(solution)/shard_map/ppermute | solution.py:286
  114.7 10.6 %collective-permute-start.15 = (f32[1,4,128,128]{3,2,1,0:T(8,128)S(1)}, f32[1,4,128,128]{3,2,1,0:T(8,128)S(1)}, u32[]{:S(2)}, u32[]{:S(2)}) collective-permute-start(f32[1,4,128,128]{3,2,1,0:T(8,128)S(1)} %get-tuple-element.17), channel_id=1, source_target_pairs={{0,4},{4,8},{8,12},{12,16},{16,20},{20,24},{24,28},{1,5},{5,9},{9,... | collective-permute-start | bytes 786440 | tf_op jit(solution)/shard_map/ppermute | solution.py:287
  (2 other events, 1.3 us)

commit v2 on v0

v2 whole, which is shorter than its diff:
```python
import functools

import jax
import jax.numpy as jnp
from jax import lax
from jax.experimental import pallas as pl
from jax.experimental.pallas import tpu as pltpu
from jax.sharding import PartitionSpec as P

UNROLL = 4
BUFFERS = 6
VMEM_LIMIT = 8 * 1024 * 1024


def split(value):
    high = value.astype(jnp.bfloat16)
    low = (value - high.astype(jnp.float32)).astype(jnp.bfloat16)
    return high, low


def work(microseconds):
    return pl.CostEstimate(flops=microseconds * 10**9, bytes_accessed=microseconds * 10**6, transcendentals=0)


def bits(count):
    return max(1, (count - 1).bit_length())


class Layout:
    def __init__(self, e_local, n_slot, p_slot, size, pat, groups, agg_slab):
        self.e_local, self.n_slot, self.p_slot, self.size, self.pat = e_local, n_slot, p_slot, size, pat
        self.groups, self.agg_slab, self.per_owner = groups, agg_slab, agg_slab // groups
        self.blocks = e_local * p_slot
        self.near_at = 0
        self.near_count_at = e_local * n_slot
        self.cols_at = self.near_count_at + e_local
        self.col_count_at = self.cols_at + self.blocks
        self.live_at = self.col_count_at + e_local
        self.longest = 2 * e_local * n_slot * p_slot * p_slot * pat + UNROLL
        self.most_q = 2 * e_local * p_slot * n_slot + 2 * UNROLL
        self.row_blocks = self.per_owner * pat
        self.outs = 6 * self.row_blocks
        self.p_bits, self.o_bits = bits(self.blocks), bits(self.outs + 1)


def list_kernel(lay, place, mine, theirs, slot_of, pattern, list_ref, count_ref, q_list, need_ref):
    row, grp = place[0], place[1]
    core = lax.bitwise_and(grp, 1)
    edge = jnp.logical_or(grp == 0, grp == lay.groups - 1)
    for b in range(BUFFERS):
        count_ref[b] = 0

    def scan(side, first_q):
        meta = (mine, theirs)[side]

        def over_e(e, q_found):
            for j in range(lay.p_slot):
                need_ref[side * lay.blocks + e * lay.p_slot + j] = 0

            def over_j(j, q_found):
                c = meta[lay.cols_at + e * lay.p_slot + j]
                slot = slot_of[c]
                owner = lax.bitwise_xor(slot // lay.per_owner, grp)
                upper = lax.shift_right_logical(owner, 1)
                slab_at = c // lay.agg_slab - row + 1
                out = ((upper * 3 + slab_at) * lay.per_owner + lax.rem(slot, lay.per_owner)) * lay.pat
                wanted = [pattern[c * lay.pat + s] for s in range(lay.pat)]
                ej = e * lay.p_slot + j
                ours = lax.bitwise_and(owner, 1) == 0
                need_ref[side * lay.blocks + ej] = ours.astype(jnp.int32)

                def over_k(k, q_found):
                    n = meta[lay.near_at + e * lay.n_slot + k]
                    home = n // lay.e_local
                    inner = n - home * lay.e_local
                    home_row = home // lay.groups
                    offset = home_row - row
                    crossed = lax.bitwise_xor(home - home_row * lay.groups, grp)
                    in_slab = offset == 0
                    rim_other = jnp.where(offset < 0, 1 - core, core)
                    other = jnp.where(in_slab, lax.bitwise_and(crossed, 1), rim_other)
                    holder_edge = jnp.logical_xor(edge, other == 1)
                    far = jnp.logical_and(in_slab, crossed >= 2)
                    rim = jnp.logical_not(in_slab)
                    late = jnp.where(holder_edge, far, rim)
                    part = jnp.where(jnp.logical_and(in_slab, crossed < 2), 0, jnp.where(late, 2, 1))
                    field = jnp.where(in_slab, lax.shift_right_logical(crossed, 1), 2)
                    buffer = part * 2 + other
                    at = inner * lay.p_slot
                    field_at = lay.live_at + field * lay.blocks + at
                    found = count_ref[buffer]
                    start = found
                    base = buffer * lay.longest
                    for l in range(lay.p_slot):
                        d = jnp.where(other == 0, mine[field_at + l], theirs[field_at + l])
                        code = ((((q_found << lay.p_bits) + at + l) << lay.o_bits) + out)
                        for s in range(lay.pat):
                            list_ref[base + found] = code + s
                            found = found + (wanted[s] == d).astype(jnp.int32)
                    count_ref[buffer] = found
                    q_list[q_found] = ej * lay.n_slot + k
                    return q_found + (found > start).astype(jnp.int32)

                live_near = jnp.where(ours, meta[lay.near_count_at + e], 0)
                return lax.fori_loop(0, live_near, over_k, q_found)

            return lax.fori_loop(0, meta[lay.col_count_at + e], over_j, q_found)

        q_found = lax.fori_loop(0, lay.e_local, over_e, first_q)
        for u in range(UNROLL):
            q_list[q_found + u] = 0
        return (q_found + UNROLL - 1) // UNROLL

    middle = scan(0, jnp.int32(0))
    count_ref[BUFFERS] = middle
    count_ref[BUFFERS + 1] = scan(1, middle * UNROLL)
    for b in range(BUFFERS):
        for u in range(UNROLL):
            list_ref[b * lay.longest + count_ref[b] + u] = lay.outs


def match_lists(lay, place, mine, theirs, coarse_slot, pattern):
    smem = pl.BlockSpec(memory_space=pltpu.SMEM)
    return pl.pallas_call(
        functools.partial(list_kernel, lay),
        in_specs=[smem] * 5,
        out_specs=[smem] * 4,
        out_shape=[
            jax.ShapeDtypeStruct((BUFFERS * lay.longest,), jnp.int32),
            jax.ShapeDtypeStruct((BUFFERS + 2,), jnp.int32),
            jax.ShapeDtypeStruct((lay.most_q + UNROLL,), jnp.int32),
            jax.ShapeDtypeStruct((2 * lay.blocks,), jnp.int32),
        ],
        compiler_params=pltpu.CompilerParams(vmem_limit_bytes=1024 * 1024),
        cost_estimate=work(4),
        name="match_lists",
    )(place, mine, theirs, coarse_slot, pattern)


def left_kernel(lay, count_ref, q_list, need_ref, a_mine, a_theirs, p_mine, p_theirs, q_ref, left_ref):
    for side, p_ref in enumerate((p_mine, p_theirs)):

        def prepare(ej, carry, side=side, p_ref=p_ref):
            @pl.when(need_ref[side * lay.blocks + ej] == 1)
            def _():
                high, low = split(p_ref[ej].T)
                left_ref[side * lay.blocks + ej] = jnp.concatenate([high, high, low], axis=1)

            return carry

        lax.fori_loop(0, lay.blocks, prepare, 0)

    def products(side, first_chunk, past_chunk):
        a_ref = (a_mine, a_theirs)[side]

        def step(chunk, carry):
            results = []
            for u in range(UNROLL):
                code = q_list[chunk * UNROLL + u]
                ej = code // lay.n_slot
                ek = (ej // lay.p_slot) * lay.n_slot + code - ej * lay.n_slot
                high, low = split(a_ref[ek])
                right = jnp.concatenate([high, low, high], axis=0)
                results.append(
                    jnp.dot(left_ref[side * lay.blocks + ej], right, preferred_element_type=jnp.float32)
                )
            for u in range(UNROLL):
                q_ref[chunk * UNROLL + u] = results[u]
            return carry

        lax.fori_loop(first_chunk, past_chunk, step, 0)

    products(0, 0, count_ref[BUFFERS])
    products(1, count_ref[BUFFERS], count_ref[BUFFERS + 1])


def left_products(lay, counts, q_list, need, a_mine, a_theirs, p_mine, p_theirs):
    smem = pl.BlockSpec(memory_space=pltpu.SMEM)
    vmem = pl.BlockSpec(memory_space=pltpu.VMEM)
    return pl.pallas_call(
        functools.partial(left_kernel, lay),
        in_specs=[smem] * 3 + [vmem] * 4,
        out_specs=vmem,
        out_shape=jax.ShapeDtypeStruct((lay.most_q, lay.size, lay.size), jnp.float32),
        scratch_shapes=[pltpu.VMEM((2 * lay.blocks, lay.size, 3 * lay.size), jnp.bfloat16)],
        compiler_params=pltpu.CompilerParams(vmem_limit_bytes=VMEM_LIMIT),
        cost_estimate=work(5),
        name="left_products",
    )(counts, q_list, need, a_mine, a_theirs, p_mine, p_theirs)


def add_matches(lay, list_ref, count_ref, q_ref, p_refs, buffers, acc):
    for b, p_ref in zip(buffers, p_refs):

        def step(chunk, carry, b=b, p_ref=p_ref):
            results, outs = [], []
            for u in range(UNROLL):
                code = list_ref[b * lay.longest + chunk * UNROLL + u]
                outs.append(lax.bitwise_and(code, (1 << lay.o_bits) - 1))
                code = lax.shift_right_logical(code, lay.o_bits)
                at = lax.bitwise_and(code, (1 << lay.p_bits) - 1)
                q_high, q_low = split(q_ref[lax.shift_right_logical(code, lay.p_bits)])
                p_high, p_low = split(p_ref[at])
                left = jnp.concatenate([q_high, q_high, q_low], axis=1)
                right = jnp.concatenate([p_high, p_low, p_high], axis=0)
                results.append(jnp.dot(left, right, preferred_element_type=jnp.float32))
            for u in range(UNROLL):
                acc[outs[u]] += results[u]
            return carry

        lax.fori_loop(0, (count_ref[b] + UNROLL - 1) // UNROLL, step, 0)


def early_kernel(lay, list_ref, count_ref, q_ref, p0, p1, p2, p3, out_ref, acc):
    for i in range(lay.outs):
        acc[i] = jnp.zeros((lay.size, lay.size), jnp.float32)
    add_matches(lay, list_ref, count_ref, q_ref, (p0, p1, p2, p3), range(4), acc)
    for i in range(lay.outs):
        out_ref[i] = acc[i]


def late_kernel(lay, list_ref, count_ref, q_ref, p4, p5, part, *refs):
    outs, acc = refs[:6], refs[6]
    for i in range(lay.outs):
        acc[i] = part[i]
    add_matches(lay, list_ref, count_ref, q_ref, (p4, p5), range(4, 6), acc)
    for t in range(6):
        for i in range(lay.row_blocks):
            outs[t][i] = acc[t * lay.row_blocks + i]


def match_sums(kernel, lay, lists, counts, q_blocks, vectors, out_shape, cost, name):
    smem = pl.BlockSpec(memory_space=pltpu.SMEM)
    vmem = pl.BlockSpec(memory_space=pltpu.VMEM)
    return pl.pallas_call(
        functools.partial(kernel, lay),
        in_specs=[smem, smem] + [vmem] * (1 + len(vectors)),
        out_specs=[vmem] * len(out_shape),
        out_shape=out_shape,
        scratch_shapes=[pltpu.VMEM((lay.outs + 1, lay.size, lay.size), jnp.float32)],
        compiler_params=pltpu.CompilerParams(vmem_limit_bytes=VMEM_LIMIT),
        cost_estimate=work(cost),
        name=name,
    )(lists, counts, q_blocks, *vectors)


def per_device(
    a_blocks, neighbours, neighbour_count, p_blocks, p_columns, p_count, coarse_slot, coarse_pattern
):
    rows, groups = lax.axis_size("rows"), lax.axis_size("grp")
    e_local, n_slot, size = a_blocks.shape[:3]
    p_slot, pat = p_blocks.shape[1], coarse_pattern.shape[1]
    lay = Layout(e_local, n_slot, p_slot, size, pat, groups, coarse_slot.shape[0] // rows)
    row, grp = lax.axis_index("rows"), lax.axis_index("grp")
    upper, first, last = groups // 2, 0, groups - 1
    both = ("rows", "grp")
    core_pairs = [(g, g ^ 1) for g in range(groups)]
    upper_pairs = [(g, g ^ upper) for g in range(groups)]
    edges, inners = [first, last], [first ^ upper, last ^ upper]

    def along(g, step):
        return [
            (r * groups + g, (r + step) * groups + g)
            for r in range(rows)
            if 0 <= r + step < rows
        ]

    is_edge = (grp == first) | (grp == last)
    live = jnp.arange(p_slot, dtype=jnp.int32)[None, :] < p_count[:, None]
    own_live = jnp.where(live, p_columns, -1).reshape(-1)
    far_live = lax.ppermute(own_live, "grp", upper_pairs)
    rim_live = lax.ppermute(
        jnp.where(is_edge, own_live, far_live),
        both,
        along(last, 1) + along(first, -1) + along(last ^ upper, 1) + along(first ^ upper, -1),
    )
    mine = jnp.concatenate(
        [neighbours.reshape(-1), neighbour_count, p_columns.reshape(-1), p_count, own_live, far_live, rim_live]
    )
    theirs = lax.ppermute(mine, "grp", core_pairs)

    own = p_blocks.reshape(lay.blocks, size, size)
    a_mine = a_blocks.reshape(e_local * n_slot, size, size)
    crossed_first = lax.ppermute(own, "grp", [(g, g ^ upper) for g in edges])
    rim_direct = lax.ppermute(own, both, along(last, 1) + along(first, -1))
    own_core = lax.ppermute(own, "grp", core_pairs)
    a_theirs = lax.ppermute(a_mine, "grp", core_pairs)
    crossed_second = lax.ppermute(own, "grp", [(g, g ^ upper) for g in inners])
    rim_forward = lax.ppermute(crossed_first, both, along(last ^ upper, 1) + along(first ^ upper, -1))
    second = jnp.where(is_edge, rim_direct, crossed_first)
    second_core = lax.ppermute(second, "grp", core_pairs)
    third = jnp.where(is_edge, crossed_second, rim_forward)
    third_core = lax.ppermute(third, "grp", core_pairs)

    place = jnp.stack([row, grp]).astype(jnp.int32)
    lists, counts, q_list, need = match_lists(lay, place, mine, theirs, coarse_slot, coarse_pattern.reshape(-1))
    q_blocks = left_products(lay, counts, q_list, need, a_mine, a_theirs, own, own_core)
    blocks = lambda count: jax.ShapeDtypeStruct((count, size, size), jnp.float32)
    (part,) = match_sums(
        early_kernel, lay, lists, counts, q_blocks, [own, own_core, second, second_core], [blocks(lay.outs)], 5, "early"
    )
    kept_down, kept_here, kept_up, send_down, send_here, send_up = match_sums(
        late_kernel, lay, lists, counts, q_blocks, [third, third_core, part], [blocks(lay.row_blocks)] * 6, 3, "late"
    )
    down = kept_down + lax.ppermute(send_down, "grp", upper_pairs)
    up = kept_up + lax.ppermute(send_up, "grp", upper_pairs)
    here = kept_here + lax.ppermute(send_here, "grp", upper_pairs)
    from_next = lax.ppermute(down, "rows", [(r, r - 1) for r in range(1, rows)])
    from_prev = lax.ppermute(up, "rows", [(r, r + 1) for r in range(rows - 1)])
    return (here + from_next + from_prev).reshape(lay.per_owner, pat, size, size)


def solution(mesh):
    return jax.shard_map(
        per_device,
        mesh=mesh,
        in_specs=(
            P(("rows", "grp"), None, None, None),
            P(("rows", "grp"), None),
            P(("rows", "grp")),
            P(("rows", "grp"), None, None, None),
            P(("rows", "grp"), None),
            P(("rows", "grp")),
            P(),
            P(),
        ),
        out_specs=P(("rows", "grp"), None, None, None),
        check_vma=False,
    )
```

time: 252 us -> 90.4 us (0.36)
  the two profiles are of different devices: /device:TPU:0 before, /device:TPU:12 now
where the time goes in v2:
time: 90.4 us; the launch traced here: 89.7 us
  waiting for transfers between devices  42.6 us (47%)
  starting transfers between devices  22.5 us (25%)
  Pallas kernels  17.9 us (20%)
  local copies, waits for them, and re-layouts  3.4 us (4%)
  other arithmetic  3.08 us (3%)
    ppermute x1, waiting for transfers between devices, per_device(): crossed_first = lax.ppermute(own, 'grp', [(g, g ^ upper) for g in edges])  14.1 us
    ppermute x1, waiting for transfers between devices, per_device(): lax.ppermute(jnp.where(is_edge, own_live, far_live), both, along(last, 1)...  7.14 us
    ppermute x1, waiting for transfers between devices, per_device(): down = kept_down + lax.ppermute(send_down, 'grp', upper_pairs)  6.76 us
    ppermute x1, starting transfers between devices, per_device(): crossed_second = lax.ppermute(own, 'grp', [(g, g ^ upper) for g in inners])  6.3 us
    pallas_call x1, Pallas kernels, match_lists(): pl.pallas_call(functools.partial(list_kernel, lay), in_specs=[smem] * 5,...  6.21 us
    ppermute x1, waiting for transfers between devices, per_device(): from_prev = lax.ppermute(up, 'rows', [(r, r + 1) for r in range(rows - 1)])  6.17 us
    pallas_call x1, Pallas kernels, left_products(): pl.pallas_call(functools.partial(left_kernel, lay), in_specs=[smem] * 3 +...  6.06 us
    pallas_call x2, Pallas kernels, match_sums(): pl.pallas_call(functools.partial(kernel, lay), in_specs=[smem, smem] + [v...  5.61 us
  transfers between devices with their start and end apart: 16, of which 7 were waited for; matrix products, arithmetic and copies ran while one was open for 6% of the time, Pallas kernels for 18%

profile of v2, /device:TPU:12, one launch (start us, length us, event | category | flops | bytes accessed | tf_op | source)
XLA Modules:
  0.0 89.7 jit_solution(16045565883525161297)
XLA Ops:
  0.0 1.4 %collective-permute-start.6 = (f32[16,128,128]{2,1,0:T(8,128)}, f32[16,128,128]{2,1,0:T(8,128)S(1)}, u32[]{:S(2)}, u32[]{:S(2)}) collective-permute-start(f32[16,128,128]{2,1,0:T(8,128)} %bitcast.6), channel_id=1, source_target_pairs={{0,2},{3,1},{4,6},{7,5},{8,10},{11,9},{12,14},{15,13},{16,18},{19,... | collective-permute-start | bytes 3145736 | tf_op jit(solution)/shard_map/ppermute | solution.py:284
  1.4 1.7 %collective-permute-start.9 = (f32[16,128,128]{2,1,0:T(8,128)}, f32[16,128,128]{2,1,0:T(8,128)}, u32[]{:S(2)}, u32[]{:S(2)}) collective-permute-start(f32[16,128,128]{2,1,0:T(8,128)} %bitcast.7), channel_id=1, source_target_pairs={{3,7},{7,11},{11,15},{15,19},{19,23},{23,27},{27,31},{4,0},{8,4},{... | collective-permute-start | bytes 3145736 | tf_op jit(solution)/shard_map/ppermute | solution.py:285
  3.1 6.3 %collective-permute-start.5 = (f32[16,128,128]{2,1,0:T(8,128)}, f32[16,128,128]{2,1,0:T(8,128)S(1)}, u32[]{:S(2)}, u32[]{:S(2)}) collective-permute-start(f32[16,128,128]{2,1,0:T(8,128)} %bitcast.8), channel_id=1, source_target_pairs={{2,0},{1,3},{6,4},{5,7},{10,8},{9,11},{14,12},{13,15},{18,16},{17,... | collective-permute-start | bytes 3145736 | tf_op jit(solution)/shard_map/ppermute | solution.py:288
  9.4 14.1 %collective-permute-done.6 = f32[16,128,128]{2,1,0:T(8,128)S(1)} collective-permute-done((f32[16,128,128]{2,1,0:T(8,128)}, f32[16,128,128]{2,1,0:T(8,128)S(1)}, u32[]{:S(2)}, u32[]{:S(2)}) %collective-permute-start.6) | collective-permute-done | bytes 1048608 | tf_op jit(solution)/shard_map/ppermute | solution.py:284
  23.5 3.2 %collective-permute-start.7 = (f32[16,128,128]{2,1,0:T(8,128)S(1)}, f32[16,128,128]{2,1,0:T(8,128)}, u32[]{:S(2)}, u32[]{:S(2)}) collective-permute-start(f32[16,128,128]{2,1,0:T(8,128)S(1)} %collective-permute-done.6), channel_id=1, source_target_pairs={{1,5},{5,9},{9,13},{13,17},{17,21},{21,25},{25,29},{6,2},{10,6},{1... | collective-permute-start | bytes 3145736 | tf_op jit(solution)/shard_map/ppermute | solution.py:289
  28.4 0.8 reshape.22
  29.2 0.8 copy.14
  29.9 1.2 %collective-permute-done = s32[16]{0:T(128)S(1)} collective-permute-done((s32[16]{0:T(128)S(1)}, s32[16]{0:T(128)S(1)}, u32[]{:S(2)}, u32[]{:S(2)}) %collective-permute-start) | collective-permute-done | bytes 96 | tf_op jit(solution)/shard_map/ppermute | solution.py:271
  31.1 1.9 %collective-permute-start.1 = (s32[16]{0:T(128)S(1)}, s32[16]{0:T(128)S(1)}, u32[]{:S(2)}, u32[]{:S(2)}) collective-permute-start(s32[16]{0:T(128)S(1)} %broadcast_select_fusion.2), channel_id=1, source_target_pairs={{3,7},{7,11},{11,15},{15,19},{19,23},{23,27},{27,31},{4,0},{8,4},{... | collective-permute-start | bytes 200 | tf_op jit(solution)/shard_map/ppermute | solution.py:272
  33.1 7.1 %collective-permute-done.1 = s32[16]{0:T(128)S(1)} collective-permute-done((s32[16]{0:T(128)S(1)}, s32[16]{0:T(128)S(1)}, u32[]{:S(2)}, u32[]{:S(2)}) %collective-permute-start.1) | collective-permute-done | bytes 96 | tf_op jit(solution)/shard_map/ppermute | solution.py:272
  41.8 1.3 %collective-permute-start.10 = (f32[16,128,128]{2,1,0:T(8,128)S(1)}, f32[16,128,128]{2,1,0:T(8,128)S(1)}, u32[]{:S(2)}, u32[]{:S(2)}) collective-permute-start(f32[16,128,128]{2,1,0:T(8,128)S(1)} %broadcast_select_fusion.p2), channel_id=1, source_target_pairs={{0,1},{1,0},{2,3},{3,2},{4,5},{5,4},{6,7},{7,6},{8,9},{9,8},{10,11... | collective-permute-start | bytes 3145736 | tf_op jit(solution)/shard_map/ppermute | solution.py:291
  43.1 1.3 %broadcast_select_fusion.1.p4 = f32[16,128,128]{2,1,0:T(8,128)S(1)} fusion(f32[16,128,128]{2,1,0:T(8,128)S(1)} %collective-permute-done.5, f32[16,128,128]{2,1,0:T(8,128)} %collective-permute-done.7, pred[]{:T(512)S(6)} %or.3), kind=kLoop, calls=%fused_computation.1 | loop fusion | flops 262144 | bytes 3145729 | tf_op jit(solution)/shard_map/jit(_where)/select_n | solution.py:292
  44.6 6.2 %match_lists.1 = (s32[10776]{0:T(1024)S(1)}, s32[8]{0:T(128)S(1)}, s32[236]{0:T(256)S(1)}, s32[32]{0:T(128)S(1)}) custom-call(s32[2]{0:T(128)S(1)} %pad_add_fusion.place, s32[136]{0:T(256)S(1)} %concatenate.3.mine, s32[136]{0:T(256)S(1)} %collective-permute-done.2.theirs, s32[32]{0:T(128)S(1)} %copy-done.2, s32[128]{0:T(128)S(1)} %reshape.25.pattern), custom_call_target="tpu_custom_call" | custom-call | flops 4000000000 | bytes 4000000 | tf_op jit(solution)/shard_map/match_lists/pallas_call | solution.py:124
  50.8 6.1 %left_products.1.q_ref = f32[232,128,128]{2,1,0:T(8,128)S(1)} custom-call(s32[8]{0:T(128)S(1)} %get-tuple-element.16.count_ref, s32[236]{0:T(256)S(1)} %get-tuple-element.17.q_list, s32[32]{0:T(128)S(1)} %get-tuple-element.18.need_ref, f32[56,128,128]{2,1,0:T(8,128)S(1)} %bitcast.13, f32[56,128,128]{2,1,0:T(8,128)} %collective-permute-done.3.a_theirs, ...), custom_call_target="tpu_custom_call" | custom-call | flops 5000000000 | bytes 5000000 | tf_op jit(solution)/shard_map/left_products/pallas_call | solution.py:180
  56.9 3.6 %early.1.part = f32[24,128,128]{2,1,0:T(8,128)S(1)} custom-call(s32[10776]{0:T(1024)S(1)} %get-tuple-element.15.list_ref, s32[8]{0:T(128)S(1)} %get-tuple-element.16.count_ref, f32[232,128,128]{2,1,0:T(8,128)S(1)} %left_products.1.q_ref, f32[16,128,128]{2,1,0:T(8,128)S(1)} %bitcast.11, f32[16,128,128]{2,1,0:T(8,128)S(1)} %collective-permute-done.4.p_theirs.p1, ...), custom_call_target="tpu_custom_call" | custom-call | flops 5000000000 | bytes 5000000 | tf_op jit(solution)/shard_map/early/pallas_call | solution.py:235
  60.5 2.0 %late.1 = (f32[4,128,128]{2,1,0:T(8,128)S(1)}, f32[4,128,128]{2,1,0:T(8,128)S(1)}, f32[4,128,128]{2,1,0:T(8,128)S(1)}, f32[4,128,128]{2,1,0:T(8,128)S(1)}, f32[4...) custom-call(s32[10776]{0:T(1024)S(1)} %get-tuple-element.15.list_ref, s32[8]{0:T(128)S(1)} %get-tuple-element.16.count_ref, ...), custom_call_target="tpu_custom_call" | custom-call | flops 3000000000 | bytes 3000000 | tf_op jit(solution)/shard_map/late/pallas_call | solution.py:235
  62.6 2.0 %collective-permute-start.14 = (f32[4,128,128]{2,1,0:T(8,128)S(1)}, f32[4,128,128]{2,1,0:T(8,128)S(1)}, u32[]{:S(2)}, u32[]{:S(2)}) collective-permute-start(f32[4,128,128]{2,1,0:T(8,128)S(1)} %get-tuple-element.24), channel_id=1, source_target_pairs={{0,2},{1,3},{2,0},{3,1},{4,6},{5,7},{6,4},{7,5},{8,10},{9,11},{10,... | collective-permute-start | bytes 786440 | tf_op jit(solution)/shard_map/ppermute | solution.py:306
  64.7 6.8 %collective-permute-done.12 = f32[4,128,128]{2,1,0:T(8,128)S(1)} collective-permute-done((f32[4,128,128]{2,1,0:T(8,128)S(1)}, f32[4,128,128]{2,1,0:T(8,128)S(1)}, u32[]{:S(2)}, u32[]{:S(2)}) %collective-permute-start.12) | collective-permute-done | bytes 262176 | tf_op jit(solution)/shard_map/ppermute | solution.py:305
  71.5 1.9 %collective-permute-start.13 = (f32[4,128,128]{2,1,0:T(8,128)S(1)}, f32[4,128,128]{2,1,0:T(8,128)S(1)}, u32[]{:S(2)}, u32[]{:S(2)}) collective-permute-start(f32[4,128,128]{2,1,0:T(8,128)S(1)} %add.16), channel_id=1, source_target_pairs={{4,0},{8,4},{12,8},{16,12},{20,16},{24,20},{28,24},{5,1},{9,5},{13... | collective-permute-start | bytes 786440 | tf_op jit(solution)/shard_map/ppermute | solution.py:308
  73.4 3.6 %collective-permute-done.14 = f32[4,128,128]{2,1,0:T(8,128)S(1)} collective-permute-done((f32[4,128,128]{2,1,0:T(8,128)S(1)}, f32[4,128,128]{2,1,0:T(8,128)S(1)}, u32[]{:S(2)}, u32[]{:S(2)}) %collective-permute-start.14) | collective-permute-done | bytes 262176 | tf_op jit(solution)/shard_map/ppermute | solution.py:306
  77.1 1.9 %collective-permute-start.15 = (f32[4,128,128]{2,1,0:T(8,128)S(1)}, f32[4,128,128]{2,1,0:T(8,128)S(1)}, u32[]{:S(2)}, u32[]{:S(2)}) collective-permute-start(f32[4,128,128]{2,1,0:T(8,128)S(1)} %add.18), channel_id=1, source_target_pairs={{0,4},{4,8},{8,12},{12,16},{16,20},{20,24},{24,28},{1,5},{5,9},{9,... | collective-permute-start | bytes 786440 | tf_op jit(solution)/shard_map/ppermute | solution.py:309
  79.1 3.6 %collective-permute-done.11 = f32[4,128,128]{2,1,0:T(8,128)S(1)} collective-permute-done((f32[4,128,128]{2,1,0:T(8,128)S(1)}, f32[4,128,128]{2,1,0:T(8,128)S(1)}, u32[]{:S(2)}, u32[]{:S(2)}) %collective-permute-start.11) | collective-permute-done | bytes 262176 | tf_op jit(solution)/shard_map/ppermute | solution.py:307
  82.7 6.2 %collective-permute-done.15 = f32[4,128,128]{2,1,0:T(8,128)S(1)} collective-permute-done((f32[4,128,128]{2,1,0:T(8,128)S(1)}, f32[4,128,128]{2,1,0:T(8,128)S(1)}, u32[]{:S(2)}, u32[]{:S(2)}) %collective-permute-start.15) | collective-permute-done | bytes 262176 | tf_op jit(solution)/shard_map/ppermute | solution.py:309
  88.9 0.8 add_bitcast_fusion
  (34 shorter events, 3.7 us)
Async XLA Ops:
  0.0 44.6 %copy-start.2 = (s32[32]{0:T(128)S(1)}, s32[32]{0:T(128)}, u32[]{:S(2)}) copy-start(s32[32]{0:T(128)} %slot_of.1) | copy-start | bytes 388
  0.0 50.8 %collective-permute-start.3 = (f32[56,128,128]{2,1,0:T(8,128)}, f32[56,128,128]{2,1,0:T(8,128)}, u32[]{:S(2)}, u32[]{:S(2)}) collective-permute-start(f32[56,128,128]{2,1,0:T(8,128)} %bitcast.12), channel_id=1, source_target_pairs={{0,1},{1,0},{2,3},{3,2},{4,5},{5,4},{6,7},{7,6},{8,9},{9,8},{10,11... | collective-permute-start | bytes 11010056 | tf_op jit(solution)/shard_map/ppermute | solution.py:287
  0.0 23.5 %collective-permute-start.6 = (f32[16,128,128]{2,1,0:T(8,128)}, f32[16,128,128]{2,1,0:T(8,128)S(1)}, u32[]{:S(2)}, u32[]{:S(2)}) collective-permute-start(f32[16,128,128]{2,1,0:T(8,128)} %bitcast.6), channel_id=1, source_target_pairs={{0,2},{3,1},{4,6},{7,5},{8,10},{11,9},{12,14},{15,13},{16,18},{19,... | collective-permute-start | bytes 3145736 | tf_op jit(solution)/shard_map/ppermute | solution.py:284
  1.4 39.7 %collective-permute-start.9 = (f32[16,128,128]{2,1,0:T(8,128)}, f32[16,128,128]{2,1,0:T(8,128)}, u32[]{:S(2)}, u32[]{:S(2)}) collective-permute-start(f32[16,128,128]{2,1,0:T(8,128)} %bitcast.7), channel_id=1, source_target_pairs={{3,7},{7,11},{11,15},{15,19},{19,23},{23,27},{27,31},{4,0},{8,4},{... | collective-permute-start | bytes 3145736 | tf_op jit(solution)/shard_map/ppermute | solution.py:285
  3.1 38.7 %collective-permute-start.5 = (f32[16,128,128]{2,1,0:T(8,128)}, f32[16,128,128]{2,1,0:T(8,128)S(1)}, u32[]{:S(2)}, u32[]{:S(2)}) collective-permute-start(f32[16,128,128]{2,1,0:T(8,128)} %bitcast.8), channel_id=1, source_target_pairs={{2,0},{1,3},{6,4},{5,7},{10,8},{9,11},{14,12},{13,15},{18,16},{17,... | collective-permute-start | bytes 3145736 | tf_op jit(solution)/shard_map/ppermute | solution.py:288
  23.5 19.6 %collective-permute-start.7 = (f32[16,128,128]{2,1,0:T(8,128)S(1)}, f32[16,128,128]{2,1,0:T(8,128)}, u32[]{:S(2)}, u32[]{:S(2)}) collective-permute-start(f32[16,128,128]{2,1,0:T(8,128)S(1)} %collective-permute-done.6), channel_id=1, source_target_pairs={{1,5},{5,9},{9,13},{13,17},{17,21},{21,25},{25,29},{6,2},{10,6},{1... | collective-permute-start | bytes 3145736 | tf_op jit(solution)/shard_map/ppermute | solution.py:289
  27.5 3.5 %collective-permute-start = (s32[16]{0:T(128)S(1)}, s32[16]{0:T(128)S(1)}, u32[]{:S(2)}, u32[]{:S(2)}) collective-permute-start(s32[16]{0:T(128)S(1)} %reshape.24), channel_id=1, source_target_pairs={{0,2},{1,3},{2,0},{3,1},{4,6},{5,7},{6,4},{7,5},{8,10},{9,11},{10,... | collective-permute-start | bytes 200 | tf_op jit(solution)/shard_map/ppermute | solution.py:271
  31.1 9.2 %collective-permute-start.1 = (s32[16]{0:T(128)S(1)}, s32[16]{0:T(128)S(1)}, u32[]{:S(2)}, u32[]{:S(2)}) collective-permute-start(s32[16]{0:T(128)S(1)} %broadcast_select_fusion.2), channel_id=1, source_target_pairs={{3,7},{7,11},{11,15},{15,19},{19,23},{23,27},{27,31},{4,0},{8,4},{... | collective-permute-start | bytes 200 | tf_op jit(solution)/shard_map/ppermute | solution.py:272
  40.3 10.5 %collective-permute-start.4 = (f32[16,128,128]{2,1,0:T(8,128)}, f32[16,128,128]{2,1,0:T(8,128)S(1)}, u32[]{:S(2)}, u32[]{:S(2)}) collective-permute-start(f32[16,128,128]{2,1,0:T(8,128)} %bitcast.9), channel_id=1, source_target_pairs={{0,1},{1,0},{2,3},{3,2},{4,5},{5,4},{6,7},{7,6},{8,9},{9,8},{10,11... | collective-permute-start | bytes 3145736 | tf_op jit(solution)/shard_map/ppermute | solution.py:286
  41.1 3.5 %collective-permute-start.2 = (s32[136]{0:T(256)S(1)}, s32[136]{0:T(256)S(1)}, u32[]{:S(2)}, u32[]{:S(2)}) collective-permute-start(s32[136]{0:T(256)S(1)} %concatenate.3.mine), channel_id=1, source_target_pairs={{0,1},{1,0},{2,3},{3,2},{4,5},{5,4},{6,7},{7,6},{8,9},{9,8},{10,11... | collective-permute-start | bytes 1640 | tf_op jit(solution)/shard_map/ppermute | solution.py:280
  41.8 15.1 %collective-permute-start.10 = (f32[16,128,128]{2,1,0:T(8,128)S(1)}, f32[16,128,128]{2,1,0:T(8,128)S(1)}, u32[]{:S(2)}, u32[]{:S(2)}) collective-permute-start(f32[16,128,128]{2,1,0:T(8,128)S(1)} %broadcast_select_fusion.p2), channel_id=1, source_target_pairs={{0,1},{1,0},{2,3},{3,2},{4,5},{5,4},{6,7},{7,6},{8,9},{9,8},{10,11... | collective-permute-start | bytes 3145736 | tf_op jit(solution)/shard_map/ppermute | solution.py:291
  44.4 6.4 %copy-start = (f32[8,2,128,128]{3,2,1,0:T(8,128)S(1)}, f32[8,2,128,128]{3,2,1,0:T(8,128)}, u32[]{:S(2)}) copy-start(f32[8,2,128,128]{3,2,1,0:T(8,128)} %param.11) | copy-start | bytes 3145732
  44.5 6.4 %copy-start.1 = (f32[8,7,128,128]{3,2,1,0:T(8,128)S(1)}, f32[8,7,128,128]{3,2,1,0:T(8,128)}, u32[]{:S(2)}) copy-start(f32[8,7,128,128]{3,2,1,0:T(8,128)} %param.8) | copy-start | bytes 11010052
  44.5 16.1 %collective-permute-start.8 = (f32[16,128,128]{2,1,0:T(8,128)S(1)}, f32[16,128,128]{2,1,0:T(8,128)S(1)}, u32[]{:S(2)}, u32[]{:S(2)}) collective-permute-start(f32[16,128,128]{2,1,0:T(8,128)S(1)} %broadcast_select_fusion.1.p4), channel_id=1, source_target_pairs={{0,1},{1,0},{2,3},{3,2},{4,5},{5,4},{6,7},{7,6},{8,9},{9,8},{10,11... | collective-permute-start | bytes 3145736 | tf_op jit(solution)/shard_map/ppermute | solution.py:293
  62.5 8.9 %collective-permute-start.12 = (f32[4,128,128]{2,1,0:T(8,128)S(1)}, f32[4,128,128]{2,1,0:T(8,128)S(1)}, u32[]{:S(2)}, u32[]{:S(2)}) collective-permute-start(f32[4,128,128]{2,1,0:T(8,128)S(1)} %get-tuple-element.22), channel_id=1, source_target_pairs={{0,2},{1,3},{2,0},{3,1},{4,6},{5,7},{6,4},{7,5},{8,10},{9,11},{10,... | collective-permute-start | bytes 786440 | tf_op jit(solution)/shard_map/ppermute | solution.py:305
  62.6 14.5 %collective-permute-start.14 = (f32[4,128,128]{2,1,0:T(8,128)S(1)}, f32[4,128,128]{2,1,0:T(8,128)S(1)}, u32[]{:S(2)}, u32[]{:S(2)}) collective-permute-start(f32[4,128,128]{2,1,0:T(8,128)S(1)} %get-tuple-element.24), channel_id=1, source_target_pairs={{0,2},{1,3},{2,0},{3,1},{4,6},{5,7},{6,4},{7,5},{8,10},{9,11},{10,... | collective-permute-start | bytes 786440 | tf_op jit(solution)/shard_map/ppermute | solution.py:306
  64.6 18.1 %collective-permute-start.11 = (f32[4,128,128]{2,1,0:T(8,128)S(1)}, f32[4,128,128]{2,1,0:T(8,128)S(1)}, u32[]{:S(2)}, u32[]{:S(2)}) collective-permute-start(f32[4,128,128]{2,1,0:T(8,128)S(1)} %get-tuple-element.20), channel_id=1, source_target_pairs={{0,2},{1,3},{2,0},{3,1},{4,6},{5,7},{6,4},{7,5},{8,10},{9,11},{10,... | collective-permute-start | bytes 786440 | tf_op jit(solution)/shard_map/ppermute | solution.py:307
  71.5 11.2 %collective-permute-start.13 = (f32[4,128,128]{2,1,0:T(8,128)S(1)}, f32[4,128,128]{2,1,0:T(8,128)S(1)}, u32[]{:S(2)}, u32[]{:S(2)}) collective-permute-start(f32[4,128,128]{2,1,0:T(8,128)S(1)} %add.16), channel_id=1, source_target_pairs={{4,0},{8,4},{12,8},{16,12},{20,16},{24,20},{28,24},{5,1},{9,5},{13... | collective-permute-start | bytes 786440 | tf_op jit(solution)/shard_map/ppermute | solution.py:308
  77.1 11.7 %collective-permute-start.15 = (f32[4,128,128]{2,1,0:T(8,128)S(1)}, f32[4,128,128]{2,1,0:T(8,128)S(1)}, u32[]{:S(2)}, u32[]{:S(2)}) collective-permute-start(f32[4,128,128]{2,1,0:T(8,128)S(1)} %add.18), channel_id=1, source_target_pairs={{0,4},{4,8},{8,12},{12,16},{16,20},{20,24},{24,28},{1,5},{5,9},{9,... | collective-permute-start | bytes 786440 | tf_op jit(solution)/shard_map/ppermute | solution.py:309
